TPU v7x, 32 devices: a whole 2x2x4 slice. The times are simulated.
32 devices in a mesh: pairs: 2 (over y), rows: 8 (over z, x), cols: 2 (over core).
Axes of the slice: x: 2, y: 2, z: 4, core: 2. Of those that a mesh axis runs over, the one named last changes fastest.
Arguments:
- left_image: bfloat16 [32, 1024, 128], P(('pairs', 'rows'), 'cols'), parts along dimension 0, may hold values from -6 to 6
- right_image: bfloat16 [32, 1024, 128], P(('pairs', 'rows'), 'cols'), parts along dimension 0, may hold values from -6 to 6
- weight: bfloat16 [1152, 256], replicated, may hold values from -0.1875 to 0.1875
- level_zero: bfloat16 [32, 1024, 256], P(('pairs', 'rows'), 'cols'), parts along dimension 0, may hold values from -6 to 6
- level_one: bfloat16 [32, 1024, 128], P(('pairs', 'rows'), 'cols'), parts along dimension 0, may hold values from -6 to 6
- level_two: bfloat16 [32, 1024, 64], P(('pairs', 'rows'), 'cols'), parts along dimension 0, may hold values from -6 to 6
- level_three: bfloat16 [32, 1024, 32], P(('pairs', 'rows'), 'cols'), parts along dimension 0, may hold values from -6 to 6
Outputs:
- grad_left_in: bfloat16 [32, 1024, 128], P(('pairs', 'rows'), 'cols'), parts along dimension 0
- grad_right_in: bfloat16 [32, 1024, 128], P(('pairs', 'rows'), 'cols'), parts along dimension 0
- weight_grad: float32 [512, 1152], P(('pairs', 'rows')), parts along dimension 0
There are 2 independent parts, one for each index of `pairs`. A program takes and returns all parts, laid end to end along the dimension named above; an argument that names none is the same for every part. Nothing has to cross between parts.
All inputs are finite; a program needn't handle non-finite values.
Results may differ from a plain program's by a relative error of at most 0.008.
Values may be sent and summed in bfloat16 or wider, within the bound.
No kernel may reach another device: no remote copies, remote signals or barrier semaphores. Data moves between devices by JAX's collectives and lax.ppermute only.
A program may use at most 64 MiB of HBM per device.

v0:
```python
import math

import jax
import jax.numpy as jnp
from jax import lax
from jax.sharding import PartitionSpec as P


def with_halo(block, sides, width):
    for axis, dim in sides:
        count = lax.axis_size(axis)
        forward = [(i, i + 1) for i in range(count - 1)]
        backward = [(target, source) for source, target in forward]
        low = lax.ppermute(
            lax.slice_in_dim(block, block.shape[dim] - width, None, axis=dim), axis, forward
        )
        high = lax.ppermute(lax.slice_in_dim(block, 0, width, axis=dim), axis, backward)
        block = jnp.concatenate([low, block, high], axis=dim)
    return block


def shifted_2(x, axis, by):
    length = lax.axis_size(axis)
    pairs = [(i, i + by) for i in range(length) if 0 <= i + by < length]
    return lax.ppermute(x, axis, pairs)


def skewed(band_rev):
    depth, count, width = band_rev.shape
    padded = jnp.pad(band_rev, ((0, 0), (0, 0), (0, count)))
    flat = padded.reshape(depth, count * (width + count))[:, : count * (width + count - 1)]
    return flat.reshape(depth, count, width + count - 1)


def combined_grad(level_zero, level_one, level_two, level_three):
    total = level_zero.astype(jnp.float32)
    total = total + jnp.repeat(level_one.astype(jnp.float32), 2, axis=-1) * 0.5
    total = total + jnp.repeat(level_two.astype(jnp.float32), 4, axis=-1) * 0.25
    total = total + jnp.repeat(level_three.astype(jnp.float32), 8, axis=-1) * 0.125
    return total.astype(jnp.bfloat16)


def on_device(left_image, right_image, weight, level_zero, level_one, level_two, level_three):
    depth, band, channels = left_image.shape
    features = weight.shape[1]
    reach = level_zero.shape[2]
    edge = reach - 1
    images = jnp.stack([left_image, right_image])
    framed = with_halo(images, (("rows", 1), ("cols", 2)), 1)
    taken_list = []
    for row_tap in range(3):
        for col_tap in range(3):
            taken_list.append(
                framed[:, row_tap : row_tap + depth, col_tap : col_tap + band].reshape(-1, channels)
            )
    patches = jnp.concatenate(taken_list, axis=1)
    feats = jnp.dot(patches, weight, preferred_element_type=jnp.float32).astype(jnp.bfloat16)
    feats = feats.reshape(2, depth, band, features)
    left_feat = feats[0]
    right_feat = feats[1]
    corr_grad = combined_grad(level_zero, level_one, level_two, level_three)
    incoming = shifted_2(right_feat[:, band - edge :], "cols", 1)
    right_ext = jnp.concatenate([incoming, right_feat], axis=1)
    ext_grad = jnp.zeros((depth, band + edge, features), jnp.float32)
    lefts = []
    for start in range(0, band, reach):
        matrix = skewed(corr_grad[:, start : start + reach, ::-1])
        window = right_ext[:, start : start + reach + edge]
        lefts.append(jnp.einsum("rik,rkc->ric", matrix, window, preferred_element_type=jnp.float32))
        block_left = left_feat[:, start : start + reach]
        ext_grad = ext_grad.at[:, start : start + reach + edge].add(
            jnp.einsum("rik,ric->rkc", matrix, block_left, preferred_element_type=jnp.float32)
        )
    returned = shifted_2(ext_grad[:, :edge].astype(jnp.bfloat16), "cols", -1).astype(jnp.float32)
    right_sum = ext_grad[:, edge:].at[:, band - edge :].add(returned)
    inverse = 1.0 / math.sqrt(features)
    left_grad = (jnp.concatenate(lefts, axis=1) * inverse).astype(jnp.bfloat16)
    right_grad = (right_sum * inverse).astype(jnp.bfloat16)
    feat_grad = jnp.stack([left_grad, right_grad])
    bordered = with_halo(feat_grad, (("rows", 1), ("cols", 2)), 1)
    back_sum = jnp.zeros((2 * depth * band, channels), jnp.float32)
    for row_tap in range(3):
        for col_tap in range(3):
            index = row_tap * 3 + col_tap
            taps_w = weight[index * channels : (index + 1) * channels]
            shifted = bordered[
                :, 2 - row_tap : 2 - row_tap + depth, 2 - col_tap : 2 - col_tap + band
            ].reshape(-1, features)
            back_sum = back_sum + lax.dot_general(
                shifted, taps_w, (((1,), (1,)), ((), ())), preferred_element_type=jnp.float32
            )
    grad_pair = back_sum.astype(jnp.bfloat16).reshape(2, depth, band, channels)
    flat_grad = feat_grad.reshape(-1, features)
    scale = 1.0 / math.sqrt(2 * depth * band * lax.axis_size("rows") * lax.axis_size("cols"))
    part = lax.psum_scatter(
        lax.dot_general(
            flat_grad, patches, (((0,), (0,)), ((), ())), preferred_element_type=jnp.float32
        )
        * scale,
        "rows",
        scatter_dimension=0,
        tiled=True,
    )
    weight_grad = lax.psum(part, "cols")
    return (grad_pair[0], grad_pair[1], weight_grad)


def solution(mesh):
    placed = (
        P(("pairs", "rows"), "cols", None),
        P(("pairs", "rows"), "cols", None),
        P(),
        P(("pairs", "rows"), "cols", None),
        P(("pairs", "rows"), "cols", None),
        P(("pairs", "rows"), "cols", None),
        P(("pairs", "rows"), "cols", None),
    )
    return jax.shard_map(
        on_device,
        mesh=mesh,
        in_specs=placed,
        out_specs=(
            P(("pairs", "rows"), "cols", None),
            P(("pairs", "rows"), "cols", None),
            P(("pairs", "rows"), None),
        ),
        check_vma=False,
    )
```

profile of v0, /device:TPU:0, one launch (start us, length us, event | category | flops | bytes accessed | tf_op | source)
XLA Modules:
  0.0 173.7 jit_solution(14971016403167053623)
XLA Ops:
  7.2 1.9 %fusion.10 = (bf16[2,1,512,128]{3,2,1,0:T(8,128)(2,1)}, bf16[2,1,512,128]{3,2,1,0:T(8,128)(2,1)S(1)}) fusion(bf16[1,2,512,128]{3,2,1,0:T(8,128)(2,1)} %bitcast.74, bf16[1,2,512,128]{3,2,1,0:T(8,128)(2,1)} %bitcast.78), kind=kLoop, calls=%fused_computation.55 | loop fusion | flops 262144 | bytes 1048576 | tf_op jit(solution)/shard_map/stack | solution.py:48
  9.1 4.8 %collective-permute-start = (bf16[2,1,512,128]{3,2,1,0:T(8,128)(2,1)}, bf16[2,1,512,128]{3,2,1,0:T(8,128)(2,1)S(1)}, u32[]{:S(2)}, u32[]{:S(2)}) collective-permute-start(bf16[2,1,512,128]{3,2,1,0:T(8,128)(2,1)} %get-tuple-element.73), channel_id=1, source_target_pairs={{0,2},{2,4},{4,6},{6,8},{8,10},{10,12},{12,14},{1,3},{3,5},{5,7},{... | collective-permute-start | bytes 786440 | tf_op jit(solution)/shard_map/ppermute | solution.py:14
  14.0 1.4 collective-permute-start.1
  15.4 0.9 convert_multiply_fusion.2
  16.7 0.5 copy.20
  17.5 1.2 fusion.4
  18.7 0.4 fusion.33
  19.5 0.5 copy.32
  20.4 1.3 reshape.213
  22.2 0.5 copy.33
  23.1 1.3 reshape.224
  24.4 1.0 collective-permute-done
  25.5 1.3 collective-permute-start.2
  26.8 1.5 collective-permute-start.3
  28.4 1.4 collective-permute-done.3
  29.8 0.5 pad_maximum_fusion.2
  30.4 0.6 fusion.29
  32.1 0.5 copy-done.5
  32.7 1.6 convolution_convert_fusion
  35.3 1.3 collective-permute-start.5
  36.7 0.8 slice.299
  37.4 3.0 %collective-permute-start.4 = (bf16[2,255,256]{2,1,0:T(8,128)(2,1)}, bf16[2,255,256]{2,1,0:T(8,128)(2,1)S(1)}, u32[]{:S(2)}, u32[]{:S(2)}) collective-permute-start(bf16[2,255,256]{2,1,0:T(8,128)(2,1)} %slice.299), channel_id=1, source_target_pairs={{0,1},{2,3},{4,5},{6,7},{8,9},{10,11},{12,13},{14,15},{16,17},{18,... | collective-permute-start | bytes 783368 | tf_op jit(solution)/shard_map/ppermute | solution.py:25
  40.5 1.1 convolution_bitcast_fusion
  41.7 2.2 %scatter-add.14 = f32[2,512,256]{2,1,0:T(8,128)S(1)} dynamic-update-slice(f32[2,512,256]{2,1,0:T(8,128)S(1)} %slice.306, f32[2,255,256]{2,1,0:T(8,128)S(1)} %slice_add_fusion, s32[]{:T(128)} %constant.93.clone.1, s32[]{:T(128)} %constant.95.clone.1, s32[]{:T(128)} %constant.93.clone.1) | dynamic-update-slice | bytes 1044484 | tf_op jit(solution)/shard_map/scatter-add | solution.py:75
  44.5 4.3 %collective-permute-start.6 = (bf16[2,1,512,256]{3,2,1,0:T(8,128)(2,1)S(1)}, bf16[2,1,512,256]{3,2,1,0:T(8,128)(2,1)S(1)}, u32[]{:S(2)}, u32[]{:S(2)}) collective-permute-start(bf16[2,1,512,256]{3,2,1,0:T(8,128)(2,1)S(1)} %get-tuple-element.58), channel_id=1, source_target_pairs={{0,2},{2,4},{4,6},{6,8},{8,10},{10,12},{12,14},{1,3},{3,5},{5,7},{... | collective-permute-start | bytes 1572872 | tf_op jit(solution)/shard_map/ppermute | solution.py:14
  48.8 1.3 collective-permute-start.7
  50.1 20.6 %collective-permute-done.6 = bf16[2,1,512,256]{3,2,1,0:T(8,128)(2,1)S(1)} collective-permute-done((bf16[2,1,512,256]{3,2,1,0:T(8,128)(2,1)S(1)}, bf16[2,1,512,256]{3,2,1,0:T(8,128)(2,1)S(1)}, u32[]{:S(2)}, u32[]{:S(2)}) %collective-permute-start.6) | collective-permute-done | bytes 524320 | tf_op jit(solution)/shard_map/ppermute | solution.py:14
  70.8 1.3 pad_maximum_fusion.3
  72.0 1.0 copy-done
  73.0 4.9 %convolution_multiply_fusion = f32[256,1152]{1,0:T(8,128)} fusion(bf16[2048,256]{1,0:T(8,128)(2,1)S(1)} %bitcast.66, bf16[2048,1152]{1,0:T(8,128)(2,1)} %copy-done.11), kind=kOutput, calls=%fused_computation | convolution fusion | flops 1208254464 | bytes 6946816 | tf_op jit(solution)/shard_map/dot_general | solution.py:96
  78.1 1.4 collective-permute-start.8
  79.5 3.0 %collective-permute-start.9 = (bf16[2,4,1,256]{3,2,1,0:T(2,128)(2,1)S(1)}, bf16[2,4,1,256]{3,2,1,0:T(2,128)(2,1)S(1)}, u32[]{:S(2)}, u32[]{:S(2)}) collective-permute-start(bf16[2,4,1,256]{3,2,1,0:T(2,128)(2,1)S(1)} %get-tuple-element.48), channel_id=1, source_target_pairs={{0,1},{2,3},{4,5},{6,7},{8,9},{10,11},{12,13},{14,15},{16,17},{18,... | collective-permute-start | bytes 12296 | tf_op jit(solution)/shard_map/ppermute | solution.py:14
  82.6 0.4 fusion.23
  83.4 2.0 %pad_maximum_fusion = (bf16[2,4,513,256]{3,2,1,0:T(8,128)(2,1)S(1)}, bf16[2,4,513,256]{3,2,1,0:T(8,128)(2,1)S(1)}) fusion(bf16[2,4,1,256]{3,2,1,0:T(2,128)(2,1)S(1)} %collective-permute-done.8, bf16[2,1,512,256]{3,2,1,0:T(8,128)(2,1)S(1)} %collective-permute-done.7, bf16[1,2,512,256]{3,2,1,0:T(8,128)(2,1)S(1)} %fusion.5, ...), kind=kLoop, calls=%fused_computation.11 | loop fusion | flops 21012480 | bytes 6307840 | tf_op jit(solution)/shard_map/concatenate | solution.py:18
  85.4 0.6 fusion.27
  86.2 0.4 fusion.15
  86.6 0.4 convolution_add_fusion.6
  87.1 0.4 convolution_add_fusion.5
  87.5 0.4 convolution_add_fusion.4
  88.0 0.8 copy-done.1
  88.7 0.4 convolution_add_fusion.3
  89.2 0.4 convolution_add_fusion.2
  89.6 0.4 convolution_add_fusion.1
  90.1 0.4 fusion.1
  90.5 55.4 %reduce-scatter.2.cloned.1.call-done = f32[32,1152]{1,0:T(8,128)} async-done(((f32[256,1152]{1,0:T(8,128)}), f32[32,1152]{1,0:T(8,128)}) %reduce-scatter.2.cloned.1.call-update) | async-done | bytes 147472 | tf_op jit(solution)/shard_map/reduce_scatter | solution.py:95
  146.0 0.8 fusion.32
  146.8 18.5 %all-reduce.5.cloned.1.call-done = f32[32,1152]{1,0:T(8,128)} async-done(((f32[32,1152]{1,0:T(8,128)}), f32[32,1152]{1,0:T(8,128)}) %all-reduce.5.cloned.1.call-update) | async-done | bytes 147472 | tf_op jit(solution)/shard_map/psum | solution.py:104
  165.3 1.6 copy.46
  (69 shorter events, 5.9 us)
Async XLA Ops:
  7.2 9.3 %copy-start.9 = (bf16[2,512,128]{2,1,0:T(8,128)(2,1)S(1)}, bf16[2,512,128]{2,1,0:T(8,128)(2,1)}, u32[]{:S(2)}) copy-start(bf16[2,512,128]{2,1,0:T(8,128)(2,1)} %param.17) | copy-start | bytes 786436
  7.2 138.8 %reduce-scatter.2.cloned.1.call-start = ((), (), s32[]{:S(2)}) async-start(), calls=%async_computation.1 | async-start | bytes 1327104 | tf_op jit(solution)/shard_map/reduce_scatter | solution.py:95
  7.2 9.5 %copy-start.8 = (bf16[2,512,256]{2,1,0:T(8,128)(2,1)S(1)}, bf16[2,512,256]{2,1,0:T(8,128)(2,1)}, u32[]{:S(2)}) copy-start(bf16[2,512,256]{2,1,0:T(8,128)(2,1)} %param.16) | copy-start | bytes 1572868
  9.1 16.3 %collective-permute-start = (bf16[2,1,512,128]{3,2,1,0:T(8,128)(2,1)}, bf16[2,1,512,128]{3,2,1,0:T(8,128)(2,1)S(1)}, u32[]{:S(2)}, u32[]{:S(2)}) collective-permute-start(bf16[2,1,512,128]{3,2,1,0:T(8,128)(2,1)} %get-tuple-element.73), channel_id=1, source_target_pairs={{0,2},{2,4},{4,6},{6,8},{8,10},{10,12},{12,14},{1,3},{3,5},{5,7},{... | collective-permute-start | bytes 786440 | tf_op jit(solution)/shard_map/ppermute | solution.py:14
  14.0 3.3 %copy-start.10 = (bf16[2,512,64]{1,2,0:T(8,128)(2,1)S(1)}, bf16[2,512,64]{1,2,0:T(8,128)(2,1)}, u32[]{:S(2)}) copy-start(bf16[2,512,64]{1,2,0:T(8,128)(2,1)} %param.18) | copy-start | bytes 393220
  14.0 11.5 %collective-permute-start.1 = (bf16[2,1,512,128]{3,2,1,0:T(8,128)(2,1)S(1)}, bf16[2,1,512,128]{3,2,1,0:T(8,128)(2,1)S(1)}, u32[]{:S(2)}, u32[]{:S(2)}) collective-permute-start(bf16[2,1,512,128]{3,2,1,0:T(8,128)(2,1)S(1)} %get-tuple-element.74), channel_id=1, source_target_pairs={{2,0},{4,2},{6,4},{8,6},{10,8},{12,10},{14,12},{3,1},{5,3},{7,5},{... | collective-permute-start | bytes 786440 | tf_op jit(solution)/shard_map/ppermute | solution.py:17
  22.0 3.5 %copy-start.3 = (bf16[2,512,128]{2,1,0:T(8,128)(2,1)S(1)}, bf16[2,512,128]{2,1,0:T(8,128)(2,1)}, u32[]{:S(2)}) copy-start(bf16[2,512,128]{2,1,0:T(8,128)(2,1)} %param.13) | copy-start | bytes 786436
  22.0 3.5 %copy-start.4 = (bf16[2,512,128]{2,1,0:T(8,128)(2,1)S(1)}, bf16[2,512,128]{2,1,0:T(8,128)(2,1)}, u32[]{:S(2)}) copy-start(bf16[2,512,128]{2,1,0:T(8,128)(2,1)} %param.14) | copy-start | bytes 786436
  25.5 2.9 %collective-permute-start.2 = (bf16[2,4,1,128]{3,2,1,0:T(2,128)(2,1)S(1)}, bf16[2,4,1,128]{3,2,1,0:T(2,128)(2,1)S(1)}, u32[]{:S(2)}, u32[]{:S(2)}) collective-permute-start(bf16[2,4,1,128]{3,2,1,0:T(2,128)(2,1)S(1)} %get-tuple-element.65), channel_id=1, source_target_pairs={{0,1},{2,3},{4,5},{6,7},{8,9},{10,11},{12,13},{14,15},{16,17},{18,... | collective-permute-start | bytes 6152 | tf_op jit(solution)/shard_map/ppermute | solution.py:14
  26.8 3.1 %collective-permute-start.3 = (bf16[2,4,1,128]{3,2,1,0:T(2,128)(2,1)S(1)}, bf16[2,4,1,128]{3,2,1,0:T(2,128)(2,1)S(1)}, u32[]{:S(2)}, u32[]{:S(2)}) collective-permute-start(bf16[2,4,1,128]{3,2,1,0:T(2,128)(2,1)S(1)} %get-tuple-element.64), channel_id=1, source_target_pairs={{1,0},{3,2},{5,4},{7,6},{9,8},{11,10},{13,12},{15,14},{17,16},{19,... | collective-permute-start | bytes 6152 | tf_op jit(solution)/shard_map/ppermute | solution.py:17
  31.6 1.1 copy-start.5
  32.7 2.1 %copy-start.11 = (bf16[2048,1152]{1,0:T(8,128)(2,1)}, bf16[2048,1152]{1,0:T(8,128)(2,1)S(1)}, u32[]{:S(2)}) copy-start(bf16[2048,1152]{1,0:T(8,128)(2,1)S(1)} %constant_dynamic-update-slice_fusion) | copy-start | bytes 14155780
  35.3 6.3 %collective-permute-start.5 = (bf16[2,255,256]{2,1,0:T(8,128)(2,1)S(1)}, bf16[2,255,256]{2,1,0:T(8,128)(2,1)S(1)}, u32[]{:S(2)}, u32[]{:S(2)}) collective-permute-start(bf16[2,255,256]{2,1,0:T(8,128)(2,1)S(1)} %slice.372), channel_id=1, source_target_pairs={{1,0},{3,2},{5,4},{7,6},{9,8},{11,10},{13,12},{15,14},{17,16},{19,... | collective-permute-start | bytes 783368 | tf_op jit(solution)/shard_map/ppermute | solution.py:25
  37.4 6.6 %collective-permute-start.4 = (bf16[2,255,256]{2,1,0:T(8,128)(2,1)}, bf16[2,255,256]{2,1,0:T(8,128)(2,1)S(1)}, u32[]{:S(2)}, u32[]{:S(2)}) collective-permute-start(bf16[2,255,256]{2,1,0:T(8,128)(2,1)} %slice.299), channel_id=1, source_target_pairs={{0,1},{2,3},{4,5},{6,7},{8,9},{10,11},{12,13},{14,15},{16,17},{18,... | collective-permute-start | bytes 783368 | tf_op jit(solution)/shard_map/ppermute | solution.py:25
  41.7 2.6 %copy-start.7 = (f32[1,2,256,256]{3,2,1,0:T(8,128)S(1)}, f32[1,2,256,256]{3,2,1,0:T(8,128)}, u32[]{:S(2)}) copy-start(f32[1,2,256,256]{3,2,1,0:T(8,128)} %convolution_bitcast_fusion) | copy-start | bytes 1572868
  44.5 26.2 %collective-permute-start.6 = (bf16[2,1,512,256]{3,2,1,0:T(8,128)(2,1)S(1)}, bf16[2,1,512,256]{3,2,1,0:T(8,128)(2,1)S(1)}, u32[]{:S(2)}, u32[]{:S(2)}) collective-permute-start(bf16[2,1,512,256]{3,2,1,0:T(8,128)(2,1)S(1)} %get-tuple-element.58), channel_id=1, source_target_pairs={{0,2},{2,4},{4,6},{6,8},{8,10},{10,12},{12,14},{1,3},{3,5},{5,7},{... | collective-permute-start | bytes 1572872 | tf_op jit(solution)/shard_map/ppermute | solution.py:14
  48.8 21.9 %collective-permute-start.7 = (bf16[2,1,512,256]{3,2,1,0:T(8,128)(2,1)S(1)}, bf16[2,1,512,256]{3,2,1,0:T(8,128)(2,1)S(1)}, u32[]{:S(2)}, u32[]{:S(2)}) collective-permute-start(bf16[2,1,512,256]{3,2,1,0:T(8,128)(2,1)S(1)} %get-tuple-element.59), channel_id=1, source_target_pairs={{2,0},{4,2},{6,4},{8,6},{10,8},{12,10},{14,12},{3,1},{5,3},{7,5},{... | collective-permute-start | bytes 1572872 | tf_op jit(solution)/shard_map/ppermute | solution.py:17
  72.0 1.0 copy-start
  78.0 87.3 %all-reduce.5.cloned.1.call-start = ((), (), s32[]{:S(2)}) async-start(), calls=%async_computation.2 | async-start | bytes 294912 | tf_op jit(solution)/shard_map/psum | solution.py:104
  78.1 4.5 %copy-start.2 = (bf16[2,2,512,256]{3,2,1,0:T(8,128)(2,1)S(1)}, bf16[2,2,512,256]{3,2,1,0:T(8,128)(2,1)}, u32[]{:S(2)}) copy-start(bf16[2,2,512,256]{3,2,1,0:T(8,128)(2,1)} %get-tuple-element.56) | copy-start | bytes 3145732
  78.1 4.5 %copy-start.6 = (bf16[1152,256]{1,0:T(8,128)(2,1)S(1)}, bf16[1152,256]{1,0:T(8,128)(2,1)}, u32[]{:S(2)}) copy-start(bf16[1152,256]{1,0:T(8,128)(2,1)} %param.15) | copy-start | bytes 1769476
  78.1 4.9 %collective-permute-start.8 = (bf16[2,4,1,256]{3,2,1,0:T(2,128)(2,1)S(1)}, bf16[2,4,1,256]{3,2,1,0:T(2,128)(2,1)S(1)}, u32[]{:S(2)}, u32[]{:S(2)}) collective-permute-start(bf16[2,4,1,256]{3,2,1,0:T(2,128)(2,1)S(1)} %get-tuple-element.47), channel_id=1, source_target_pairs={{1,0},{3,2},{5,4},{7,6},{9,8},{11,10},{13,12},{15,14},{17,16},{19,... | collective-permute-start | bytes 12296 | tf_op jit(solution)/shard_map/ppermute | solution.py:17
  79.5 3.8 %collective-permute-start.9 = (bf16[2,4,1,256]{3,2,1,0:T(2,128)(2,1)S(1)}, bf16[2,4,1,256]{3,2,1,0:T(2,128)(2,1)S(1)}, u32[]{:S(2)}, u32[]{:S(2)}) collective-permute-start(bf16[2,4,1,256]{3,2,1,0:T(2,128)(2,1)S(1)} %get-tuple-element.48), channel_id=1, source_target_pairs={{0,1},{2,3},{4,5},{6,7},{8,9},{10,11},{12,13},{14,15},{16,17},{18,... | collective-permute-start | bytes 12296 | tf_op jit(solution)/shard_map/ppermute | solution.py:14
  87.5 1.2 copy-start.1
Sparse Core Ops, SparseCore 0:
  78.1 67.7 reduce-scatter.1
  148.2 16.9 all-reduce.4
where the time goes:
time: 174 us
  waiting for transfers between devices  97.4 us (56%)
  starting transfers between devices  23.5 us (14%)
  local copies, waits for them, and re-layouts  17.3 us (10%)
  between operations  14.7 us (8%)
  matrix products  12.5 us (7%)
  other arithmetic  8.28 us (5%)
    reduce_scatter x1, waiting for transfers between devices, on_device(): lax.psum_scatter(lax.dot_general(flat_grad, patches, (((0,), (0,)), ((),...  55.4 us
    ppermute x4, waiting for transfers between devices, with_halo(): lax.ppermute(lax.slice_in_dim(block, block.shape[dim] - width, None, axis...  22 us
    psum x1, waiting for transfers between devices, on_device(): weight_grad = lax.psum(part, 'cols')  18.5 us
    ppermute x4, starting transfers between devices, with_halo(): lax.ppermute(lax.slice_in_dim(block, block.shape[dim] - width, None, axis...  13.5 us
    unnamed x40, local copies, waits for them, and re-layouts  7.06 us
    ppermute x4, starting transfers between devices, with_halo(): lax.ppermute(lax.slice_in_dim(block, 0, width, axis=dim), axis, backward)  5.61 us
    dot_general x1, matrix products, on_device(): lax.dot_general(flat_grad, patches, (((0,), (0,)), ((), ())), preferred_e...  4.94 us
    ppermute x2, starting transfers between devices, shifted_2(): return lax.ppermute(x, axis, pairs)  4.34 us
  transfers between devices with their start and end apart: 12, of which 6 were waited for; matrix products, arithmetic and copies ran while one was open for 12% of the time, Pallas kernels for 0%

commit v1 on v0

v1 whole, which is shorter than its diff:
```python
import math

import jax
import jax.numpy as jnp
from jax import lax
from jax.experimental import pallas as pl
from jax.experimental.pallas import tpu as pltpu
from jax.sharding import PartitionSpec as P

BF = jnp.bfloat16
F32 = jnp.float32
MIB = 1 << 20
PAD = 8


def dot(a, b):
    return jnp.dot(a, b, preferred_element_type=F32)


def vmem(count):
    return [pl.BlockSpec(memory_space=pltpu.VMEM)] * count


SCALAR = pl.BlockSpec(memory_space=pltpu.SMEM)


def shape(dims, dtype):
    return jax.ShapeDtypeStruct(dims, dtype)


def params(mib):
    return pltpu.CompilerParams(vmem_limit_bytes=mib * MIB)


def payload_kernel(core, left, right, own, near, sems):
    c = core[0]
    copies = []
    for target, row in ((own, c), (near, 1 - c)):
        for image, source in enumerate((left, right)):
            copies.append(
                pltpu.make_async_copy(source.at[row], target.at[image], sems.at[len(copies)])
            )
    for copy in copies:
        copy.start()
    for copy in copies:
        copy.wait()


def levels_kernel(core, zero, one, two, three, keep, send):
    c = core[0]
    reach = zero.shape[2]

    def spread(factor):
        source = lax.broadcasted_iota(jnp.int32, (reach // factor, reach), 0)
        target = lax.broadcasted_iota(jnp.int32, (reach // factor, reach), 1)
        first = source * factor
        inside = (target >= first) & (target < first + factor)
        return jnp.where(inside, 1.0 / factor, 0.0).astype(BF)

    a = lax.broadcasted_iota(jnp.int32, (reach, reach), 0)
    b = lax.broadcasted_iota(jnp.int32, (reach, reach), 1)
    mirror = jnp.where(a + b == reach - 1, 1.0, 0.0).astype(BF)
    for target, row in ((keep, c), (send, 1 - c)):
        total = zero[row].astype(F32)
        total = total + dot(one[row], spread(2))
        total = total + dot(two[row], spread(4))
        total = total + dot(three[row], spread(8))
        target[...] = dot(total.astype(BF), mirror).astype(BF)


def shifted_3(scratch, size):
    return jnp.concatenate(
        [scratch[pl.ds(PAD + by, size)].astype(BF) for by in (-1, 0, 1)], axis=1
    )


def clear_pads(scratch, size):
    zeros = jnp.zeros((PAD, scratch.shape[1]), F32)
    scratch[pl.ds(0, PAD)] = zeros
    scratch[pl.ds(PAD + size, PAD)] = zeros


def prepare_kernel(
    core, left, right, left_got, right_got, corr, corr_got, weight,
    own_sum, images_t, band, band_t, taps, padded, rows,
):
    c = core[0]
    half = left.shape[1]
    size = 2 * half
    channels = left.shape[2]
    features = weight.shape[2]
    reach = corr.shape[1]
    here = pl.multiple_of(c * half, half)
    there = pl.multiple_of((1 - c) * half, half)
    inner_tap = 2 - 2 * c
    outer_tap = 2 * c
    clear_pads(padded, size)
    for image, (mine, got) in enumerate(((left, left_got), (right, right_got))):
        total = None
        for role, (row, tap) in enumerate(((c, 1), (1 - c, inner_tap))):
            padded[pl.ds(PAD + here, half)] = mine[row].astype(F32)
            padded[pl.ds(PAD + there, half)] = got[row].astype(F32)
            images_t[image, pl.ds(role * channels, channels)] = (
                padded[pl.ds(PAD, size)].T.astype(BF)
            )
            part = dot(shifted_3(padded, size), weight[tap])
            total = part if total is None else total + part
        own_sum[image] = total
    rows[pl.ds(here, half)] = corr[...]
    rows[pl.ds(there, half)] = corr_got[...]
    for block in range(size // reach):
        values = rows[pl.ds(block * reach, reach)].astype(F32)
        wide = jnp.concatenate([values, jnp.zeros_like(values)], axis=1)
        skewed = pltpu.roll(wide, 1, 1, stride=1, stride_axis=0)
        band[block] = skewed.astype(BF)
        band_t[block] = skewed.T.astype(BF)
    for place, tap in enumerate((outer_tap, 1, inner_tap)):
        for col in range(3):
            piece = weight[tap, pl.ds(col * channels, channels)].astype(F32)
            taps[pl.ds(col * features, features), pl.ds(place * channels, channels)] = (
                piece.T.astype(BF)
            )


def main_kernel(
    core, halo_same, halo_other, weight, own_sum, images_t, band, band_t, taps,
    edge_same, edge_other, wg_keep, wg_send, in_keep, in_send,
    padded, feats, wide, grads, wg,
):
    c = core[0]
    half = halo_same.shape[1]
    size = 2 * half
    channels = halo_same.shape[2]
    features = feats.shape[2]
    blocks, reach = band.shape[0], band.shape[1]
    here = pl.multiple_of(c * half, half)
    there = pl.multiple_of((1 - c) * half, half)
    outer_tap = 2 * c
    inverse = 1.0 / math.sqrt(features)
    clear_pads(padded, size)
    clear_pads(wide, size)
    halo_t = []
    for image in range(2):
        padded[pl.ds(PAD + here, half)] = halo_same[image].astype(F32)
        padded[pl.ds(PAD + there, half)] = halo_other[image].astype(F32)
        halo_t.append(padded[pl.ds(PAD, size)].T.astype(BF))
        feats[image] = (
            own_sum[image] + dot(shifted_3(padded, size), weight[outer_tap])
        ).astype(BF)
    for image in range(2):
        for block in range(blocks):
            low = pl.ds(block * reach, reach)
            if image == 0:
                total = dot(band[block, :, pl.ds(reach, reach)], feats[1, low])
                if block:
                    total = total + dot(
                        band[block, :, pl.ds(0, reach)], feats[1, pl.ds((block - 1) * reach, reach)]
                    )
            else:
                total = dot(band_t[block, pl.ds(reach, reach)], feats[0, low])
                if block + 1 < blocks:
                    total = total + dot(
                        band_t[block + 1, pl.ds(0, reach)],
                        feats[0, pl.ds((block + 1) * reach, reach)],
                    )
            wide[pl.ds(PAD + block * reach, reach)] = total * inverse
        for index, by in enumerate((1, 0, -1)):
            grads[image, :, pl.ds(index * features, features)] = (
                wide[pl.ds(PAD + by, size)].astype(BF)
            )
        edge = dot(grads[image], taps[:, pl.ds(0, channels)])
        padded[pl.ds(PAD, size)] = edge
        edge_same[image] = padded[pl.ds(PAD + here, half)].astype(BF)
        edge_other[image] = padded[pl.ds(PAD + there, half)].astype(BF)
    for image in range(2):
        both = dot(grads[image], taps[:, pl.ds(channels, 2 * channels)])
        for role, row in ((0, c), (1, 1 - c)):
            padded[pl.ds(PAD, size)] = both[:, role * channels : (role + 1) * channels]
            in_keep[image, row] = padded[pl.ds(PAD + here, half)].astype(in_keep.dtype)
            in_send[image, row] = padded[pl.ds(PAD + there, half)].astype(BF)
    inner = None
    outer = None
    for image in range(2):
        part = dot(images_t[image], grads[image])
        inner = part if inner is None else inner + part
        part = dot(halo_t[image], grads[image])
        outer = part if outer is None else outer + part
    own_wg = inner[:channels].T
    inner_wg = inner[channels:].T
    outer_wg = outer.T
    first = c == 0
    wg[:, pl.ds(0, channels)] = jnp.where(first, outer_wg, inner_wg)
    wg[:, pl.ds(channels, channels)] = own_wg
    wg[:, pl.ds(2 * channels, channels)] = jnp.where(first, inner_wg, outer_wg)
    if wg_keep.shape == wg.shape:
        wg_keep[...] = wg[...]
        return
    chunks = wg_keep.shape[0]
    piece = features // chunks // 2
    for col in range(3):
        for chunk in range(chunks):
            start = col * features + chunk * 2 * piece
            rows = pl.ds(col * piece, piece)
            wg_keep[chunk, rows] = wg[
                pl.ds(pl.multiple_of(start + c * piece, piece), piece)
            ].astype(wg_keep.dtype)
            wg_send[chunk, rows] = wg[
                pl.ds(pl.multiple_of(start + (1 - c) * piece, piece), piece)
            ].astype(wg_send.dtype)


def add_kernel(keep, got, out):
    out[...] = (keep[...].astype(F32) + got[...].astype(F32)).astype(BF)


def sum_kernel(scale, parts, out):
    total = parts[0].astype(F32)
    for index in range(1, parts.shape[0]):
        total = total + parts[index].astype(F32)
    out[...] = total * scale


def finish_weight_kernel(core, mine, got, out):
    c = core[0]
    piece = mine.shape[0] // 3
    channels = mine.shape[1] // 3
    for source, place in ((mine, c), (got, 1 - c)):
        rows = pl.ds(pl.multiple_of(place * piece, piece), piece)
        for tap in range(3):
            for col in range(3):
                out[rows, pl.ds((tap * 3 + col) * channels, channels)] = source[
                    pl.ds(col * piece, piece), pl.ds(tap * channels, channels)
                ]


def finish_kernel(core, keep, got, edge_same, edge_other, left, right):
    c = core[0]
    for image, out in enumerate((left, right)):
        for row, edge in ((c, edge_other), (1 - c, edge_same)):
            out[row] = (
                keep[image, row].astype(F32)
                + got[image, row].astype(F32)
                + edge[image].astype(F32)
            ).astype(BF)


def on_device(left_image, right_image, weight, level_zero, level_one, level_two, level_three):
    depth, band, channels = left_image.shape
    features = weight.shape[1]
    reach = level_zero.shape[2]
    cores = lax.axis_size("cols")
    chips = lax.axis_size("rows")
    size = band * cores
    blocks = size // reach
    core = lax.axis_index("cols").astype(jnp.int32).reshape(1)
    swap = [(i, cores - 1 - i) for i in range(cores)]
    same_in, same_out, other = [], [], []
    for chip in range(chips - 1):
        low = chip * cores
        high = low + cores
        same_in += [(low, high), (high + 1, low + 1)]
        same_out += [(high, low), (low + 1, high + 1)]
        other += [(low + 1, high), (high, low + 1)]
    flat = ("rows", "cols")

    row_shape = shape((2, band, channels), BF)
    pay_other, pay_same = pl.pallas_call(
        payload_kernel,
        out_shape=(row_shape, row_shape),
        in_specs=[SCALAR] + [pl.BlockSpec(memory_space=pl.ANY)] * 2,
        out_specs=[pl.BlockSpec(memory_space=pl.ANY)] * 2,
        scratch_shapes=[pltpu.SemaphoreType.DMA((4,))],
    )(core, left_image, right_image)
    halo_other = lax.ppermute(pay_other, flat, other)
    halo_same = lax.ppermute(pay_same, flat, same_in)
    left_got = lax.ppermute(left_image, "cols", swap)
    right_got = lax.ppermute(right_image, "cols", swap)

    corr, corr_send = pl.pallas_call(
        levels_kernel,
        out_shape=(shape((band, reach), BF),) * 2,
        in_specs=[SCALAR] + vmem(4),
        out_specs=vmem(2),
        compiler_params=params(16),
    )(core, level_zero, level_one, level_two, level_three)
    corr_got = lax.ppermute(corr_send, "cols", swap)

    weight_3 = weight.reshape(3, 3 * channels, features)
    own_sum, images_t, skew, skew_t, taps = pl.pallas_call(
        prepare_kernel,
        out_shape=(
            shape((2, size, features), F32),
            shape((2, 2 * channels, size), BF),
            shape((blocks, reach, 2 * reach), BF),
            shape((blocks, 2 * reach, reach), BF),
            shape((3 * features, 3 * channels), BF),
        ),
        in_specs=[SCALAR] + vmem(7),
        out_specs=vmem(5),
        scratch_shapes=[
            pltpu.VMEM((size + 2 * PAD, channels), F32),
            pltpu.VMEM((size, reach), BF),
        ],
        compiler_params=params(32),
    )(core, left_image, right_image, left_got, right_got, corr, corr_got, weight_3)

    piece = features // chips // cores
    tiled = piece % 16 == 0
    wg_shape = (chips, 3 * piece, 3 * channels)
    wg_outs = (shape(wg_shape, F32), shape(wg_shape, BF))
    if not tiled:
        wg_outs = (shape((3 * features, 3 * channels), F32), shape((16, 128), BF))
    edge_same, edge_other, wg_keep, wg_send, in_keep, in_send = pl.pallas_call(
        main_kernel,
        out_shape=(
            row_shape,
            row_shape,
            *wg_outs,
            shape((2, depth, band, channels), F32),
            shape((2, depth, band, channels), BF),
        ),
        in_specs=[SCALAR] + vmem(8),
        out_specs=vmem(6),
        scratch_shapes=[
            pltpu.VMEM((size + 2 * PAD, channels), F32),
            pltpu.VMEM((2, size, features), BF),
            pltpu.VMEM((size + 2 * PAD, features), F32),
            pltpu.VMEM((2, size, 3 * features), BF),
            pltpu.VMEM((3 * features, 3 * channels), F32),
        ],
        compiler_params=params(40),
    )(core, halo_same, halo_other, weight_3, own_sum, images_t, skew, skew_t, taps)

    got_other = lax.ppermute(edge_other, flat, other)
    got_same = lax.ppermute(edge_same, flat, same_out)
    if not tiled:
        halves = wg_keep.reshape(3, chips, cores, piece, 3 * channels).transpose(2, 1, 0, 3, 4)
        halves = halves.reshape(cores, *wg_shape)
        wg_keep = lax.dynamic_index_in_dim(halves, core[0], 0, False)
        wg_send = lax.dynamic_index_in_dim(halves, cores - 1 - core[0], 0, False).astype(BF)
    wg_got = lax.ppermute(wg_send, "cols", swap)
    in_got = lax.ppermute(in_send, "cols", swap)
    chip_wg = pl.pallas_call(
        add_kernel,
        out_shape=shape(wg_send.shape, BF),
        in_specs=vmem(2),
        out_specs=vmem(1)[0],
        compiler_params=params(16),
    )(wg_keep, wg_got)
    parts = lax.all_to_all(chip_wg, "rows", 0, 0, tiled=False)
    scale = 1.0 / math.sqrt(2 * depth * band * chips * cores)
    mine = pl.pallas_call(
        lambda *refs: sum_kernel(scale, *refs),
        out_shape=shape(wg_send.shape[1:], F32),
        in_specs=vmem(1),
        out_specs=vmem(1)[0],
        compiler_params=params(16),
    )(parts)
    theirs = lax.ppermute(mine, "cols", swap)
    if tiled:
        weight_grad = pl.pallas_call(
            finish_weight_kernel,
            out_shape=shape((2 * piece, 9 * channels), F32),
            in_specs=[SCALAR] + vmem(2),
            out_specs=vmem(1)[0],
            compiler_params=params(16),
        )(core, mine, theirs)
    else:
        first = core[0] == 0
        both = jnp.stack([jnp.where(first, mine, theirs), jnp.where(first, theirs, mine)])
        both = both.reshape(cores, 3, piece, 3, channels).transpose(0, 2, 3, 1, 4)
        weight_grad = both.reshape(cores * piece, 9 * channels)
    grad_left, grad_right = pl.pallas_call(
        finish_kernel,
        out_shape=(shape(left_image.shape, BF),) * 2,
        in_specs=[SCALAR] + vmem(4),
        out_specs=vmem(2),
        compiler_params=params(16),
    )(core, in_keep, in_got, got_same, got_other)
    return grad_left, grad_right, weight_grad


def solution(mesh):
    block = P(("pairs", "rows"), "cols", None)
    return jax.shard_map(
        on_device,
        mesh=mesh,
        in_specs=(block, block, P(), block, block, block, block),
        out_specs=(block, block, P(("pairs", "rows"), None)),
        check_vma=False,
    )
```

time: 174 us -> 73 us (0.42)
  the two profiles are of different devices: /device:TPU:0 before, /device:TPU:21 now
where the time goes in v1:
time: 73 us; the launch traced here: 72.6 us
  Pallas kernels  27.2 us (37%)
  starting transfers between devices  21 us (29%)
  waiting for transfers between devices  19.5 us (27%)
  local copies, waits for them, and re-layouts  4.17 us (6%)
  between operations  0.81 us (1%)
    pallas_call x1, Pallas kernels, on_device(): pl.pallas_call(payload_kernel, out_shape=(row_shape, row_shape), in_specs...  17 us
    ppermute x1, waiting for transfers between devices, on_device(): halo_same = lax.ppermute(pay_same, flat, same_in)  5.74 us
    all_to_all x1, starting transfers between devices, on_device(): parts = lax.all_to_all(chip_wg, 'rows', 0, 0, tiled=False)  5.42 us
    ppermute x1, waiting for transfers between devices, on_device(): got_other = lax.ppermute(edge_other, flat, other)  5.01 us
    pallas_call x1, Pallas kernels, on_device(): pl.pallas_call(main_kernel, out_shape=(row_shape, row_shape, *wg_outs, sh...  4.75 us
    ppermute x1, waiting for transfers between devices, on_device(): got_same = lax.ppermute(edge_same, flat, same_out)  4.32 us
    unnamed x12, local copies, waits for them, and re-layouts  4.17 us
    ppermute x1, starting transfers between devices, on_device(): halo_other = lax.ppermute(pay_other, flat, other)  3.53 us
  transfers between devices with their start and end apart: 11, of which 6 were waited for; matrix products, arithmetic and copies ran while one was open for 0% of the time, Pallas kernels for 27%

profile of v1, /device:TPU:21, one launch (start us, length us, event | category | flops | bytes accessed | tf_op | source)
XLA Modules:
  0.0 72.6 jit_solution(2312753330997706505)
XLA Ops:
  0.6 0.0 copy-start.1
  0.6 0.0 copy-start.2
  0.7 0.0 copy-start
  0.7 1.2 %copy.10.two = bf16[2,512,64]{2,1,0:T(8,128)(2,1)S(1)} copy(bf16[2,512,64]{1,2,0:T(8,128)(2,1)} %param.12) | data formatting | bytes 262144 | tf_op args[5]
  1.8 1.0 %copy.11.three = bf16[2,512,32]{2,1,0:T(8,128)(2,1)S(1)} copy(bf16[2,512,32]{1,2,0:T(8,128)(2,1)} %param.13) | data formatting | bytes 131072 | tf_op args[6]
  2.9 0.0 copy-start.3
  2.9 1.0 %copy-done.3 = bf16[2,512,256]{2,1,0:T(8,128)(2,1)S(1)} copy-done((bf16[2,512,256]{2,1,0:T(8,128)(2,1)S(1)}, bf16[2,512,256]{2,1,0:T(8,128)(2,1)}, u32[]{:S(2)}) %copy-start.3) | copy-done | bytes 524312
  3.9 0.0 copy-start.4
  3.9 0.9 %copy-done.4 = bf16[2,512,128]{2,1,0:T(8,128)(2,1)S(1)} copy-done((bf16[2,512,128]{2,1,0:T(8,128)(2,1)S(1)}, bf16[2,512,128]{2,1,0:T(8,128)(2,1)}, u32[]{:S(2)}) %copy-start.4) | copy-done | bytes 262168
  4.8 1.2 %shard_map.95 = (bf16[512,256]{1,0:T(8,128)(2,1)S(1)}, bf16[512,256]{1,0:T(8,128)(2,1)S(1)}) custom-call(s32[1]{0:T(128)} %bitcast.core, bf16[2,512,256]{2,1,0:T(8,128)(2,1)S(1)} %copy-done.3, bf16[2,512,128]{2,1,0:T(8,128)(2,1)S(1)} %copy-done.4, bf16[2,512,64]{2,1,0:T(8,128)(2,1)S(1)} %copy.10.two, bf16[2,512,32]{2,1,0:T(8,128)(2,1)S(1)} %copy.11.three), custom_call_target="tpu_custom_call" | custom-call | tf_op jit(solution)/shard_map/pallas_call | solution.py:279
  6.1 0.7 %collective-permute-start.4 = (bf16[512,256]{1,0:T(8,128)(2,1)S(1)}, bf16[512,256]{1,0:T(8,128)(2,1)S(1)}, u32[]{:S(2)}, u32[]{:S(2)}) collective-permute-start(bf16[512,256]{1,0:T(8,128)(2,1)S(1)} %get-tuple-element.23), channel_id=1, source_target_pairs={{0,1},{1,0},{2,3},{3,2},{4,5},{5,4},{6,7},{7,6},{8,9},{9,8},{10,11... | collective-permute-start | bytes 786440 | tf_op jit(solution)/shard_map/ppermute | solution.py:286
  6.8 0.1 collective-permute-start.2
  6.9 0.4 collective-permute-start.3
  7.3 17.0 %shard_map.94 = (bf16[2,512,128]{2,1,0:T(8,128)(2,1)}, bf16[2,512,128]{2,1,0:T(8,128)(2,1)}) custom-call(s32[1]{0:T(128)} %bitcast.core, bf16[2,512,128]{2,1,0:T(8,128)(2,1)} %left.3, bf16[2,512,128]{2,1,0:T(8,128)(2,1)} %right.3), custom_call_target="tpu_custom_call" | custom-call | tf_op jit(solution)/shard_map/pallas_call | solution.py:267
  24.3 3.0 %collective-permute-start = (bf16[2,512,128]{2,1,0:T(8,128)(2,1)}, bf16[2,512,128]{2,1,0:T(8,128)(2,1)S(1)}, u32[]{:S(2)}, u32[]{:S(2)}) collective-permute-start(bf16[2,512,128]{2,1,0:T(8,128)(2,1)} %get-tuple-element.20), channel_id=1, source_target_pairs={{0,2},{3,1},{2,4},{5,3},{4,6},{7,5},{6,8},{9,7},{8,10},{11,9},{10,... | collective-permute-start | bytes 786440 | tf_op jit(solution)/shard_map/ppermute | solution.py:275
  27.3 3.5 %collective-permute-start.1 = (bf16[2,512,128]{2,1,0:T(8,128)(2,1)}, bf16[2,512,128]{2,1,0:T(8,128)(2,1)S(1)}, u32[]{:S(2)}, u32[]{:S(2)}) collective-permute-start(bf16[2,512,128]{2,1,0:T(8,128)(2,1)} %get-tuple-element.21), channel_id=1, source_target_pairs={{1,2},{2,1},{3,4},{4,3},{5,6},{6,5},{7,8},{8,7},{9,10},{10,9},{11,... | collective-permute-start | bytes 786440 | tf_op jit(solution)/shard_map/ppermute | solution.py:274
  30.9 0.0 collective-permute-done.4.corr_got
  30.9 0.0 collective-permute-done.2.left_got
  30.9 0.0 collective-permute-done.3.right_got
  30.9 0.0 copy-done.1
  30.9 0.0 copy-done.2
  30.9 0.0 copy-done
  30.9 1.8 %shard_map.96 = (f32[2,1024,256]{2,1,0:T(8,128)S(1)}, bf16[2,256,1024]{2,1,0:T(8,128)(2,1)S(1)}, bf16[4,256,512]{2,1,0:T(8,128)(2,1)S(1)}, bf16[4,512,256]{2,1,0:T(8,128)(2,1)S(1)}, bf16[768,384]{1,0:T(8,128)(2,1)S(1)}) custom-call(s32[1]{0:T(128)} %bitcast.core, bf16[2,512,128]{2,1,0:T(8,128)(2,1)S(1)} %copy-done.1, bf16[2,512,128]{2,1,0:T(8,128)(2,1)S(1)} %copy-done.2, ...), custom_call_target="tpu_custom_call" | custom-call | tf_op jit(solution)/shard_map/pallas_call | solution.py:289
  32.7 5.7 %collective-permute-done.halo_same = bf16[2,512,128]{2,1,0:T(8,128)(2,1)S(1)} collective-permute-done((bf16[2,512,128]{2,1,0:T(8,128)(2,1)}, bf16[2,512,128]{2,1,0:T(8,128)(2,1)S(1)}, u32[]{:S(2)}, u32[]{:S(2)}) %collective-permute-start) | collective-permute-done | bytes 262176 | tf_op jit(solution)/shard_map/ppermute | solution.py:275
  38.5 1.6 %collective-permute-done.1.halo_other = bf16[2,512,128]{2,1,0:T(8,128)(2,1)S(1)} collective-permute-done((bf16[2,512,128]{2,1,0:T(8,128)(2,1)}, bf16[2,512,128]{2,1,0:T(8,128)(2,1)S(1)}, u32[]{:S(2)}, u32[]{:S(2)}) %collective-permute-start.1) | collective-permute-done | bytes 262176 | tf_op jit(solution)/shard_map/ppermute | solution.py:274
  40.1 4.8 %shard_map.97 = (bf16[2,512,128]{2,1,0:T(8,128)(2,1)}, bf16[2,512,128]{2,1,0:T(8,128)(2,1)S(1)}, f32[8,48,384]{2,1,0:T(8,128)S(1)}, bf16[8,48,384]{2,1,0:T(8,128...) custom-call(s32[1]{0:T(128)} %bitcast.core, ...), custom_call_target="tpu_custom_call" | custom-call | tf_op jit(solution)/shard_map/pallas_call | solution.py:313
  44.8 0.1 collective-permute-start.8
  44.9 1.6 %collective-permute-done.8.got = bf16[8,48,384]{2,1,0:T(8,128)(2,1)S(1)} collective-permute-done((bf16[8,48,384]{2,1,0:T(8,128)(2,1)S(1)}, bf16[8,48,384]{2,1,0:T(8,128)(2,1)S(1)}, u32[]{:S(2)}, u32[]{:S(2)}) %collective-permute-start.8) | collective-permute-done | bytes 294944 | tf_op jit(solution)/shard_map/ppermute | solution.py:341
  46.5 0.8 %shard_map.99 = bf16[8,48,384]{2,1,0:T(8,128)(2,1)} custom-call(f32[8,48,384]{2,1,0:T(8,128)S(1)} %get-tuple-element.35.keep, bf16[8,48,384]{2,1,0:T(8,128)(2,1)S(1)} %collective-permute-done.8.got), custom_call_target="tpu_custom_call" | custom-call | tf_op jit(solution)/shard_map/pallas_call | solution.py:343
  47.3 5.4 %all-to-all-start = ((bf16[8,48,384]{2,1,0:T(8,128)(2,1)}), bf16[8,48,384]{2,1,0:T(8,128)(2,1)S(1)}, u32[]{:S(2)}, u32[]{:S(2)}) async-start(bf16[8,48,384]{2,1,0:T(8,128)(2,1)} %shard_map.99), calls=%async_computation | async-start | bytes 589824 | tf_op jit(solution)/shard_map/all_to_all | solution.py:350
  52.7 0.9 %collective-permute-start.5 = (bf16[2,2,512,128]{3,2,1,0:T(8,128)(2,1)S(1)}, bf16[2,2,512,128]{3,2,1,0:T(8,128)(2,1)S(1)}, u32[]{:S(2)}, u32[]{:S(2)}) collective-permute-start(bf16[2,2,512,128]{3,2,1,0:T(8,128)(2,1)S(1)} %get-tuple-element.30), channel_id=1, source_target_pairs={{0,1},{1,0},{2,3},{3,2},{4,5},{5,4},{6,7},{7,6},{8,9},{9,8},{10,11... | collective-permute-start | bytes 1572872 | tf_op jit(solution)/shard_map/ppermute | solution.py:342
  53.6 3.1 %collective-permute-start.6 = (bf16[2,512,128]{2,1,0:T(8,128)(2,1)}, bf16[2,512,128]{2,1,0:T(8,128)(2,1)S(1)}, u32[]{:S(2)}, u32[]{:S(2)}) collective-permute-start(bf16[2,512,128]{2,1,0:T(8,128)(2,1)} %get-tuple-element.31), channel_id=1, source_target_pairs={{2,0},{1,3},{4,2},{3,5},{6,4},{5,7},{8,6},{7,9},{10,8},{9,11},{12,... | collective-permute-start | bytes 786440 | tf_op jit(solution)/shard_map/ppermute | solution.py:335
  56.7 2.4 %collective-permute-start.7 = (bf16[2,512,128]{2,1,0:T(8,128)(2,1)S(1)}, bf16[2,512,128]{2,1,0:T(8,128)(2,1)S(1)}, u32[]{:S(2)}, u32[]{:S(2)}) collective-permute-start(bf16[2,512,128]{2,1,0:T(8,128)(2,1)S(1)} %get-tuple-element.32), channel_id=1, source_target_pairs={{1,2},{2,1},{3,4},{4,3},{5,6},{6,5},{7,8},{8,7},{9,10},{10,9},{11,... | collective-permute-start | bytes 786440 | tf_op jit(solution)/shard_map/ppermute | solution.py:334
  59.1 1.2 %all-to-all-done.refs_0_ = bf16[8,48,384]{2,1,0:T(8,128)(2,1)S(1)} async-done(((bf16[8,48,384]{2,1,0:T(8,128)(2,1)}), bf16[8,48,384]{2,1,0:T(8,128)(2,1)S(1)}, u32[]{:S(2)}, u32[]{:S(2)}) %all-to-all-start) | async-done | bytes 294944 | tf_op jit(solution)/shard_map/all_to_all | solution.py:350
  60.4 1.3 %collective-permute-start.9 = (f32[48,384]{1,0:T(8,128)S(1)}, f32[48,384]{1,0:T(8,128)S(1)}, u32[]{:S(2)}, u32[]{:S(2)}) collective-permute-start(f32[48,384]{1,0:T(8,128)S(1)} %shard_map.100.mine), channel_id=1, source_target_pairs={{0,1},{1,0},{2,3},{3,2},{4,5},{5,4},{6,7},{7,6},{8,9},{9,8},{10,11... | collective-permute-start | bytes 221192 | tf_op jit(solution)/shard_map/ppermute | solution.py:359
  61.7 4.3 %collective-permute-done.6.edge_same = bf16[2,512,128]{2,1,0:T(8,128)(2,1)S(1)} collective-permute-done((bf16[2,512,128]{2,1,0:T(8,128)(2,1)}, bf16[2,512,128]{2,1,0:T(8,128)(2,1)S(1)}, u32[]{:S(2)}, u32[]{:S(2)}) %collective-permute-start.6) | collective-permute-done | bytes 262176 | tf_op jit(solution)/shard_map/ppermute | solution.py:335
  66.0 5.0 %collective-permute-done.7.edge_other = bf16[2,512,128]{2,1,0:T(8,128)(2,1)S(1)} collective-permute-done((bf16[2,512,128]{2,1,0:T(8,128)(2,1)S(1)}, bf16[2,512,128]{2,1,0:T(8,128)(2,1)S(1)}, u32[]{:S(2)}, u32[]{:S(2)}) %collective-permute-start.7) | collective-permute-done | bytes 262176 | tf_op jit(solution)/shard_map/ppermute | solution.py:334
  71.0 0.0 collective-permute-done.5.got
  71.0 0.9 %shard_map.98 = (bf16[2,512,128]{2,1,0:T(8,128)(2,1)}, bf16[2,512,128]{2,1,0:T(8,128)(2,1)}) custom-call(s32[1]{0:T(128)} %bitcast.core, f32[2,2,512,128]{3,2,1,0:T(8,128)S(1)} %get-tuple-element.29.keep, bf16[2,2,512,128]{3,2,1,0:T(8,128)(2,1)S(1)} %collective-permute-done.5.got, bf16[2,512,128]{2,1,0:T(8,128)(2,1)S(1)} %collective-permute-done.6.edge_same, ...), custom_call_target="tpu_custom_call" | custom-call | tf_op jit(solution)/shard_map/pallas_call | solution.py:373
  71.9 0.0 collective-permute-done.9.got
  71.9 0.7 shard_map.101
  (1 shorter events, 0.0 us)
Async XLA Ops:
  0.6 30.3 %copy-start.1 = (bf16[2,512,128]{2,1,0:T(8,128)(2,1)S(1)}, bf16[2,512,128]{2,1,0:T(8,128)(2,1)}, u32[]{:S(2)}) copy-start(bf16[2,512,128]{2,1,0:T(8,128)(2,1)} %left.3) | copy-start | bytes 786436
  0.6 30.3 %copy-start.2 = (bf16[2,512,128]{2,1,0:T(8,128)(2,1)S(1)}, bf16[2,512,128]{2,1,0:T(8,128)(2,1)}, u32[]{:S(2)}) copy-start(bf16[2,512,128]{2,1,0:T(8,128)(2,1)} %right.3) | copy-start | bytes 786436
  0.7 30.3 %copy-start = (bf16[1152,256]{1,0:T(8,128)(2,1)S(1)}, bf16[1152,256]{1,0:T(8,128)(2,1)}, u32[]{:S(2)}) copy-start(bf16[1152,256]{1,0:T(8,128)(2,1)} %param.9) | copy-start | bytes 1769476
  2.9 1.0 %copy-start.3 = (bf16[2,512,256]{2,1,0:T(8,128)(2,1)S(1)}, bf16[2,512,256]{2,1,0:T(8,128)(2,1)}, u32[]{:S(2)}) copy-start(bf16[2,512,256]{2,1,0:T(8,128)(2,1)} %zero.1) | copy-start | bytes 1572868
  3.9 0.9 %copy-start.4 = (bf16[2,512,128]{2,1,0:T(8,128)(2,1)S(1)}, bf16[2,512,128]{2,1,0:T(8,128)(2,1)}, u32[]{:S(2)}) copy-start(bf16[2,512,128]{2,1,0:T(8,128)(2,1)} %one.1) | copy-start | bytes 786436
  6.1 24.8 %collective-permute-start.4 = (bf16[512,256]{1,0:T(8,128)(2,1)S(1)}, bf16[512,256]{1,0:T(8,128)(2,1)S(1)}, u32[]{:S(2)}, u32[]{:S(2)}) collective-permute-start(bf16[512,256]{1,0:T(8,128)(2,1)S(1)} %get-tuple-element.23), channel_id=1, source_target_pairs={{0,1},{1,0},{2,3},{3,2},{4,5},{5,4},{6,7},{7,6},{8,9},{9,8},{10,11... | collective-permute-start | bytes 786440 | tf_op jit(solution)/shard_map/ppermute | solution.py:286
  6.8 24.1 %collective-permute-start.2 = (bf16[2,512,128]{2,1,0:T(8,128)(2,1)}, bf16[2,512,128]{2,1,0:T(8,128)(2,1)S(1)}, u32[]{:S(2)}, u32[]{:S(2)}) collective-permute-start(bf16[2,512,128]{2,1,0:T(8,128)(2,1)} %left.3), channel_id=1, source_target_pairs={{0,1},{1,0},{2,3},{3,2},{4,5},{5,4},{6,7},{7,6},{8,9},{9,8},{10,11... | collective-permute-start | bytes 786440 | tf_op jit(solution)/shard_map/ppermute | solution.py:276
  6.9 24.0 %collective-permute-start.3 = (bf16[2,512,128]{2,1,0:T(8,128)(2,1)}, bf16[2,512,128]{2,1,0:T(8,128)(2,1)S(1)}, u32[]{:S(2)}, u32[]{:S(2)}) collective-permute-start(bf16[2,512,128]{2,1,0:T(8,128)(2,1)} %right.3), channel_id=1, source_target_pairs={{0,1},{1,0},{2,3},{3,2},{4,5},{5,4},{6,7},{7,6},{8,9},{9,8},{10,11... | collective-permute-start | bytes 786440 | tf_op jit(solution)/shard_map/ppermute | solution.py:277
  24.3 14.1 %collective-permute-start = (bf16[2,512,128]{2,1,0:T(8,128)(2,1)}, bf16[2,512,128]{2,1,0:T(8,128)(2,1)S(1)}, u32[]{:S(2)}, u32[]{:S(2)}) collective-permute-start(bf16[2,512,128]{2,1,0:T(8,128)(2,1)} %get-tuple-element.20), channel_id=1, source_target_pairs={{0,2},{3,1},{2,4},{5,3},{4,6},{7,5},{6,8},{9,7},{8,10},{11,9},{10,... | collective-permute-start | bytes 786440 | tf_op jit(solution)/shard_map/ppermute | solution.py:275
  27.3 12.7 %collective-permute-start.1 = (bf16[2,512,128]{2,1,0:T(8,128)(2,1)}, bf16[2,512,128]{2,1,0:T(8,128)(2,1)S(1)}, u32[]{:S(2)}, u32[]{:S(2)}) collective-permute-start(bf16[2,512,128]{2,1,0:T(8,128)(2,1)} %get-tuple-element.21), channel_id=1, source_target_pairs={{1,2},{2,1},{3,4},{4,3},{5,6},{6,5},{7,8},{8,7},{9,10},{10,9},{11,... | collective-permute-start | bytes 786440 | tf_op jit(solution)/shard_map/ppermute | solution.py:274
  44.8 1.6 %collective-permute-start.8 = (bf16[8,48,384]{2,1,0:T(8,128)(2,1)S(1)}, bf16[8,48,384]{2,1,0:T(8,128)(2,1)S(1)}, u32[]{:S(2)}, u32[]{:S(2)}) collective-permute-start(bf16[8,48,384]{2,1,0:T(8,128)(2,1)S(1)} %get-tuple-element.36), channel_id=1, source_target_pairs={{0,1},{1,0},{2,3},{3,2},{4,5},{5,4},{6,7},{7,6},{8,9},{9,8},{10,11... | collective-permute-start | bytes 884744 | tf_op jit(solution)/shard_map/ppermute | solution.py:341
  47.3 13.0 %all-to-all-start = ((bf16[8,48,384]{2,1,0:T(8,128)(2,1)}), bf16[8,48,384]{2,1,0:T(8,128)(2,1)S(1)}, u32[]{:S(2)}, u32[]{:S(2)}) async-start(bf16[8,48,384]{2,1,0:T(8,128)(2,1)} %shard_map.99), calls=%async_computation | async-start | bytes 589824 | tf_op jit(solution)/shard_map/all_to_all | solution.py:350
  52.7 18.3 %collective-permute-start.5 = (bf16[2,2,512,128]{3,2,1,0:T(8,128)(2,1)S(1)}, bf16[2,2,512,128]{3,2,1,0:T(8,128)(2,1)S(1)}, u32[]{:S(2)}, u32[]{:S(2)}) collective-permute-start(bf16[2,2,512,128]{3,2,1,0:T(8,128)(2,1)S(1)} %get-tuple-element.30), channel_id=1, source_target_pairs={{0,1},{1,0},{2,3},{3,2},{4,5},{5,4},{6,7},{7,6},{8,9},{9,8},{10,11... | collective-permute-start | bytes 1572872 | tf_op jit(solution)/shard_map/ppermute | solution.py:342
  53.6 12.4 %collective-permute-start.6 = (bf16[2,512,128]{2,1,0:T(8,128)(2,1)}, bf16[2,512,128]{2,1,0:T(8,128)(2,1)S(1)}, u32[]{:S(2)}, u32[]{:S(2)}) collective-permute-start(bf16[2,512,128]{2,1,0:T(8,128)(2,1)} %get-tuple-element.31), channel_id=1, source_target_pairs={{2,0},{1,3},{4,2},{3,5},{6,4},{5,7},{8,6},{7,9},{10,8},{9,11},{12,... | collective-permute-start | bytes 786440 | tf_op jit(solution)/shard_map/ppermute | solution.py:335
  56.7 14.3 %collective-permute-start.7 = (bf16[2,512,128]{2,1,0:T(8,128)(2,1)S(1)}, bf16[2,512,128]{2,1,0:T(8,128)(2,1)S(1)}, u32[]{:S(2)}, u32[]{:S(2)}) collective-permute-start(bf16[2,512,128]{2,1,0:T(8,128)(2,1)S(1)} %get-tuple-element.32), channel_id=1, source_target_pairs={{1,2},{2,1},{3,4},{4,3},{5,6},{6,5},{7,8},{8,7},{9,10},{10,9},{11,... | collective-permute-start | bytes 786440 | tf_op jit(solution)/shard_map/ppermute | solution.py:334
  60.4 11.6 %collective-permute-start.9 = (f32[48,384]{1,0:T(8,128)S(1)}, f32[48,384]{1,0:T(8,128)S(1)}, u32[]{:S(2)}, u32[]{:S(2)}) collective-permute-start(f32[48,384]{1,0:T(8,128)S(1)} %shard_map.100.mine), channel_id=1, source_target_pairs={{0,1},{1,0},{2,3},{3,2},{4,5},{5,4},{6,7},{7,6},{8,9},{9,8},{10,11... | collective-permute-start | bytes 221192 | tf_op jit(solution)/shard_map/ppermute | solution.py:359

commit v2 on v1

v2 whole, which is shorter than its diff:
```python
import functools
import math

import jax
import jax.numpy as jnp
from jax import lax
from jax.experimental import pallas as pl
from jax.experimental.pallas import tpu as pltpu
from jax.sharding import PartitionSpec as P

BF = jnp.bfloat16
F32 = jnp.float32
MIB = 1 << 20
PAD = 8


def dot(a, b):
    return jnp.dot(a, b, preferred_element_type=F32)


def vmem(count):
    return [pl.BlockSpec(memory_space=pltpu.VMEM)] * count


SCALAR = pl.BlockSpec(memory_space=pltpu.SMEM)


def shape(dims, dtype):
    return jax.ShapeDtypeStruct(dims, dtype)


SMALL = pl.CostEstimate(flops=1, bytes_accessed=1, transcendentals=0)


LARGE = pl.CostEstimate(flops=10**11, bytes_accessed=1, transcendentals=0)


def params(mib):
    return pltpu.CompilerParams(vmem_limit_bytes=mib * MIB)


def first_kernel(core, left, right, own, near, sems):
    c = core[0]
    copies = []
    for target, row in ((own, c), (near, 1 - c)):
        for image, source in enumerate((left, right)):
            copies.append(
                pltpu.make_async_copy(source.at[row], target.at[image], sems.at[len(copies)])
            )
    for copy in copies:
        copy.start()
    for copy in copies:
        copy.wait()


def spread(factor, reach):
    source = lax.broadcasted_iota(jnp.int32, (reach // factor, reach), 0)
    target = lax.broadcasted_iota(jnp.int32, (reach // factor, reach), 1)
    first = source * factor
    inside = (target >= first) & (target < first + factor)
    return jnp.where(inside, 1.0 / factor, 0.0).astype(BF)


def mirrored(zero, one, two_t, three_t):
    reach = zero.shape[1]
    a = lax.broadcasted_iota(jnp.int32, (reach, reach), 0)
    b = lax.broadcasted_iota(jnp.int32, (reach, reach), 1)
    mirror = jnp.where(a + b == reach - 1, 1.0, 0.0).astype(BF)
    total = zero.astype(F32)
    total = total + dot(one, spread(2, reach))
    total = total + dot(two_t.astype(F32).T.astype(BF), spread(4, reach))
    total = total + dot(three_t.astype(F32).T.astype(BF), spread(8, reach))
    return dot(total.astype(BF), mirror).astype(BF)


def shifted_3(scratch, size):
    return jnp.concatenate(
        [scratch[pl.ds(PAD + by, size)].astype(BF) for by in (-1, 0, 1)], axis=1
    )


def clear_pads(scratch, size):
    zeros = jnp.zeros((PAD, scratch.shape[1]), F32)
    scratch[pl.ds(0, PAD)] = zeros
    scratch[pl.ds(PAD + size, PAD)] = zeros


def started(moves, sems):
    copies = [
        pltpu.make_async_copy(source, target, sems.at[index])
        for index, (source, target) in enumerate(moves)
    ]
    for copy in copies:
        copy.start()
    return copies


def local_kernel(
    core, weight_hbm, zero_hbm, one_hbm, two_hbm, three_hbm,
    corr, taps, outer_weight,
    weight, zero, one, two, three, sems,
):
    c = core[0]
    copies = started(
        (
            (weight_hbm, weight),
            (zero_hbm.at[c], zero),
            (one_hbm.at[c], one),
            (two_hbm.at[c], two),
            (three_hbm.at[c], three),
        ),
        sems,
    )
    features = weight.shape[2]
    channels = weight.shape[1] // 3
    copies[0].wait()
    for place, tap in enumerate((2 * c, 1, 2 - 2 * c)):
        for col in range(3):
            piece = weight[tap, pl.ds(col * channels, channels)].astype(F32)
            taps[pl.ds(col * features, features), pl.ds(place * channels, channels)] = (
                piece.T.astype(BF)
            )
    outer_weight[...] = weight[2 * c]
    for copy in copies[1:]:
        copy.wait()
    corr[...] = mirrored(zero[...], one[...], two[...], three[...])


def prepare_kernel(
    core, left, right, left_got, right_got, zero_got, one_got, two_got, three_got, weight_hbm,
    corr,
    own_sum, images_t, band, band_t,
    padded, rows, images, weight, zero, one, two, three, sems,
):
    c = core[0]
    half = left.shape[1]
    size = 2 * half
    channels = left.shape[2]
    reach = corr.shape[1]
    here = pl.multiple_of(c * half, half)
    there = pl.multiple_of((1 - c) * half, half)
    moves = [
        (zero_got.at[c], zero),
        (one_got.at[c], one),
        (two_got.at[c], two),
        (three_got.at[c], three),
    ]
    for image, (mine, got) in enumerate(((left, left_got), (right, right_got))):
        for role, row in enumerate((c, 1 - c)):
            moves.append((mine.at[row], images.at[image, role, pl.ds(here, half)]))
            moves.append((got.at[row], images.at[image, role, pl.ds(there, half)]))
    moves.append((weight_hbm, weight))
    copies = started(moves, sems)
    clear_pads(padded, size)
    rows[pl.ds(here, half)] = corr[...]
    for copy in copies[:4]:
        copy.wait()
    rows[pl.ds(there, half)] = mirrored(zero[...], one[...], two[...], three[...])
    for copy in copies[4:]:
        copy.wait()
    for image in range(2):
        total = None
        for role, tap in enumerate((1, 2 - 2 * c)):
            whole = images[image, role].astype(F32)
            padded[pl.ds(PAD, size)] = whole
            images_t[image, pl.ds(role * channels, channels)] = whole.T.astype(BF)
            part = dot(shifted_3(padded, size), weight[tap])
            total = part if total is None else total + part
        own_sum[image] = total
    for block in range(size // reach):
        values = rows[pl.ds(block * reach, reach)].astype(F32)
        wide = jnp.concatenate([values, jnp.zeros_like(values)], axis=1)
        skewed = pltpu.roll(wide, 1, 1, stride=1, stride_axis=0)
        band[block] = skewed.astype(BF)
        band_t[block] = skewed.T.astype(BF)


def at_end(chips, chip, upper):
    return chip == jnp.where(upper, chips - 1, 0)


def main_kernel(
    chips, core, chip, halo_same, halo_other, weight, own_sum, images_t, band, band_t, taps,
    whole_grad, edge_same, edge_other, wg_keep, across,
    padded, feats, wide, grads, wg, edges, pair, edge_sems,
):
    c = core[0]
    half = halo_same.shape[1]
    size = 2 * half
    channels = halo_same.shape[2]
    features = feats.shape[2]
    blocks, reach = band.shape[0], band.shape[1]
    here = pl.multiple_of(c * half, half)
    there = pl.multiple_of((1 - c) * half, half)
    inverse = 1.0 / math.sqrt(features)
    alone = at_end(chips, chip[0], c == 1)
    clear_pads(padded, size)
    clear_pads(wide, size)
    halo_t = []
    for image in range(2):
        for place, halo in ((here, halo_same), (there, halo_other)):
            padded[pl.ds(PAD + place, half)] = jnp.where(alone, 0.0, halo[image].astype(F32))
        halo_t.append(padded[pl.ds(PAD, size)].T.astype(BF))
        feats[image] = (
            own_sum[image] + dot(shifted_3(padded, size), weight[...])
        ).astype(BF)
    for image in range(2):
        for block in range(blocks):
            low = pl.ds(block * reach, reach)
            if image == 0:
                total = dot(band[block, :, pl.ds(reach, reach)], feats[1, low])
                if block:
                    total = total + dot(
                        band[block, :, pl.ds(0, reach)], feats[1, pl.ds((block - 1) * reach, reach)]
                    )
            else:
                total = dot(band_t[block, pl.ds(reach, reach)], feats[0, low])
                if block + 1 < blocks:
                    total = total + dot(
                        band_t[block + 1, pl.ds(0, reach)],
                        feats[0, pl.ds((block + 1) * reach, reach)],
                    )
            wide[pl.ds(PAD + block * reach, reach)] = total * inverse
        for index, by in enumerate((1, 0, -1)):
            grads[image, :, pl.ds(index * features, features)] = (
                wide[pl.ds(PAD + by, size)].astype(BF)
            )
        whole_grad[image] = grads[image, :, pl.ds(features, features)]
        padded[pl.ds(PAD, size)] = dot(grads[image], taps[:, pl.ds(0, channels)])
        for index, (place, out) in enumerate(((here, edge_same), (there, edge_other))):
            edges[index, image] = padded[pl.ds(PAD + place, half)].astype(BF)
            pltpu.make_async_copy(
                edges.at[index, image], out.at[image], edge_sems.at[2 * image + index]
            ).start()
    inner = None
    outer = None
    for image in range(2):
        part = dot(images_t[image], grads[image])
        inner = part if inner is None else inner + part
        part = dot(halo_t[image], grads[image])
        outer = part if outer is None else outer + part
    for image in range(2):
        for index, out in enumerate((edge_same, edge_other)):
            pltpu.make_async_copy(
                edges.at[index, image], out.at[image], edge_sems.at[2 * image + index]
            ).wait()
    own_wg = inner[:channels].T
    inner_wg = inner[channels:].T
    outer_wg = outer.T
    first = c == 0
    wg[:, pl.ds(0, channels)] = jnp.where(first, outer_wg, inner_wg)
    wg[:, pl.ds(channels, channels)] = own_wg
    wg[:, pl.ds(2 * channels, channels)] = jnp.where(first, inner_wg, outer_wg)
    for image in range(2):
        pair[...] = dot(grads[image], taps[:, pl.ds(channels, 2 * channels)])
        for role, row in ((0, c), (1, 1 - c)):
            lanes = pl.ds(role * channels, channels)
            across[2 * image + row] = pair[pl.ds(there, half), lanes].astype(BF)
    if wg_keep.shape == wg.shape:
        wg_keep[...] = wg[...]
        return
    chunks = wg_keep.shape[0]
    piece = features // chunks // 2
    for col in range(3):
        for chunk in range(chunks):
            start = col * features + chunk * 2 * piece
            wg_keep[chunk, pl.ds(col * piece, piece)] = wg[
                pl.ds(pl.multiple_of(start + c * piece, piece), piece)
            ]
            other = wg[pl.ds(pl.multiple_of(start + (1 - c) * piece, piece), piece)].astype(BF)
            for tap in range(3):
                across[4 + tap, pl.ds((chunk * 3 + col) * piece, piece)] = (
                    other[:, tap * channels : (tap + 1) * channels]
                )


def add_kernel(keep, across, out):
    chunks, rows, lanes = keep.shape
    for chunk in range(chunks):
        for tap in range(3):
            part = pl.ds(tap * lanes // 3, lanes // 3)
            out[chunk, :, part] = (
                keep[chunk, :, part] + across[4 + tap, pl.ds(chunk * rows, rows)].astype(F32)
            ).astype(BF)


def sum_kernel(scale, parts, _, out):
    total = parts[0].astype(F32)
    for index in range(1, parts.shape[0]):
        total = total + parts[index].astype(F32)
    out[...] = total * scale


def finish_weight_kernel(core, mine, got, out):
    c = core[0]
    piece = mine.shape[0] // 3
    channels = mine.shape[1] // 3
    for source, place in ((mine, c), (got, 1 - c)):
        rows = pl.ds(pl.multiple_of(place * piece, piece), piece)
        for tap in range(3):
            for col in range(3):
                out[rows, pl.ds((tap * 3 + col) * channels, channels)] = source[
                    pl.ds(col * piece, piece), pl.ds(tap * channels, channels)
                ]


def finish_kernel(
    chips, core, chip, whole_grad, taps, across, edge_same, edge_other,
    left, right, token,
    wide, part,
):
    c = core[0]
    half, channels = left.shape[1], left.shape[2]
    size = whole_grad.shape[1]
    here = pl.multiple_of(c * half, half)
    other_alone = at_end(chips, chip[0], c == 1)
    same_alone = at_end(chips, chip[0], c == 0)
    clear_pads(wide, size)
    for image, out in enumerate((left, right)):
        wide[pl.ds(PAD, size)] = whole_grad[image].astype(F32)
        part[...] = wide[pl.ds(here, half + 2 * PAD)]
        grads = jnp.concatenate(
            [part[pl.ds(PAD + by, half)].astype(BF) for by in (1, 0, -1)], axis=1
        )
        pair = dot(grads, taps[:, pl.ds(channels, 2 * channels)])
        for role, row, edge, alone in (
            (0, c, edge_other, other_alone),
            (1, 1 - c, edge_same, same_alone),
        ):
            out[row] = (
                pair[:, role * channels : (role + 1) * channels]
                + across[2 * image + row].astype(F32)
                + jnp.where(alone, 0.0, edge[image].astype(F32))
            ).astype(BF)
    token[...] = jnp.zeros_like(token)


def on_device(left_image, right_image, weight, level_zero, level_one, level_two, level_three):
    depth, band, channels = left_image.shape
    features = weight.shape[1]
    reach = level_zero.shape[2]
    cores = lax.axis_size("cols")
    chips = lax.axis_size("rows")
    size = band * cores
    blocks = size // reach
    core = lax.axis_index("cols").astype(jnp.int32).reshape(1)
    chip_at = lax.axis_index("rows").astype(jnp.int32).reshape(1)
    swap = [(i, cores - 1 - i) for i in range(cores)]
    parts_count = lax.axis_size("pairs")
    flat = ("pairs", "rows", "cols")
    same_in, same_out, other = [], [], []
    for part in range(parts_count):
        base = part * chips * cores
        for chip in range(chips - 1):
            low = base + chip * cores
            high = low + cores
            same_in += [(low, high), (high + 1, low + 1)]
            same_out += [(high, low), (low + 1, high + 1)]
            other += [(low + 1, high), (high, low + 1)]
        first = base
        last = base + (chips - 1) * cores
        same_in += [(last, last + 1), (first + 1, first)]
        same_out += [(last + 1, last), (first, first + 1)]
        across = (part ^ 1) if parts_count % 2 == 0 else part
        away = (across - part) * chips * cores
        other += [(first, first + away), (last + 1, last + 1 + away)]

    row_shape = shape((2, band, channels), BF)
    params_in = (
        left_image,
        right_image,
        level_zero,
        level_one,
        level_two.transpose(0, 2, 1),
        level_three.transpose(0, 2, 1),
        weight.reshape(3, 3 * channels, features),
    )
    in_hbm = [pltpu.with_memory_space_constraint(x, pltpu.HBM) for x in params_in]
    any_space = pl.BlockSpec(memory_space=pl.ANY)
    own, near = pl.pallas_call(
        first_kernel,
        out_shape=(row_shape, row_shape),
        in_specs=[SCALAR] + [any_space] * 2,
        out_specs=vmem(2),
        scratch_shapes=[pltpu.SemaphoreType.DMA((4,))],
        cost_estimate=SMALL,
        compiler_params=params(2),
    )(core, *in_hbm[:2])
    halo_other = lax.ppermute(own, flat, other)
    halo_same = lax.ppermute(near, flat, same_in)
    from_core = lax.optimization_barrier((own, *params_in))[1:]
    got = [
        pltpu.with_memory_space_constraint(lax.ppermute(x, "cols", swap), pltpu.HBM)
        for x in from_core[:6]
    ]

    corr, taps, outer_weight = pl.pallas_call(
        local_kernel,
        out_shape=(
            shape((band, reach), BF),
            shape((3 * features, 3 * channels), BF),
            shape((3 * channels, features), BF),
        ),
        in_specs=[SCALAR] + [any_space] * 5,
        out_specs=vmem(3),
        scratch_shapes=[
            pltpu.VMEM((3, 3 * channels, features), BF),
            pltpu.VMEM((band, reach), BF),
            pltpu.VMEM((band, reach // 2), BF),
            pltpu.VMEM((reach // 4, band), BF),
            pltpu.VMEM((reach // 8, band), BF),
            pltpu.SemaphoreType.DMA((5,)),
        ],
        cost_estimate=LARGE,
        compiler_params=params(8),
    )(core, in_hbm[6], *in_hbm[2:6])
    own_sum, images_t, skew, skew_t = pl.pallas_call(
        prepare_kernel,
        out_shape=(
            shape((2, size, features), F32),
            shape((2, 2 * channels, size), BF),
            shape((blocks, reach, 2 * reach), BF),
            shape((blocks, 2 * reach, reach), BF),
        ),
        in_specs=[SCALAR] + [any_space] * 9 + vmem(1),
        out_specs=vmem(4),
        scratch_shapes=[
            pltpu.VMEM((size + 2 * PAD, channels), F32),
            pltpu.VMEM((size, reach), BF),
            pltpu.VMEM((2, 2, size, channels), BF),
            pltpu.VMEM((3, 3 * channels, features), BF),
            pltpu.VMEM((band, reach), BF),
            pltpu.VMEM((band, reach // 2), BF),
            pltpu.VMEM((reach // 4, band), BF),
            pltpu.VMEM((reach // 8, band), BF),
            pltpu.SemaphoreType.DMA((13,)),
        ],
        cost_estimate=SMALL,
        compiler_params=params(12),
    )(core, *in_hbm[:2], *got, in_hbm[6], corr)

    piece = features // chips // cores
    tiled = piece % 16 == 0
    wg_shape = (chips, 3 * piece, 3 * channels)
    wg_out = shape(wg_shape if tiled else (3 * features, 3 * channels), F32)
    across_shape = (7 if tiled else 4, max(band, 3 * piece * chips), channels)
    whole_grad, edge_same, edge_other, wg_keep, across = pl.pallas_call(
        functools.partial(main_kernel, chips),
        out_shape=(
            shape((2, size, features), BF),
            pltpu.HBM(row_shape.shape, BF),
            pltpu.HBM(row_shape.shape, BF),
            wg_out,
            shape(across_shape, BF),
        ),
        in_specs=[SCALAR] * 2 + vmem(8),
        out_specs=vmem(1) + [any_space] * 2 + vmem(2),
        scratch_shapes=[
            pltpu.VMEM((size + 2 * PAD, channels), F32),
            pltpu.VMEM((2, size, features), BF),
            pltpu.VMEM((size + 2 * PAD, features), F32),
            pltpu.VMEM((2, size, 3 * features), BF),
            pltpu.VMEM((3 * features, 3 * channels), F32),
            pltpu.VMEM((2, *row_shape.shape), BF),
            pltpu.VMEM((size, 2 * channels), F32),
            pltpu.SemaphoreType.DMA((4,)),
        ],
        cost_estimate=SMALL,
        compiler_params=params(16),
    )(core, chip_at, halo_same, halo_other, outer_weight, own_sum, images_t, skew, skew_t, taps)

    got_other = lax.ppermute(edge_other, flat, other)
    got_same = lax.ppermute(edge_same, flat, same_out)
    across_got = lax.ppermute(across, "cols", swap)
    if tiled:
        chip_wg = pl.pallas_call(
            add_kernel,
            out_shape=shape(wg_shape, BF),
            in_specs=vmem(2),
            out_specs=vmem(1)[0],
            cost_estimate=SMALL,
            compiler_params=params(4),
        )(wg_keep, across_got)
    else:
        halves = wg_keep.reshape(3, chips, cores, piece, 3 * channels).transpose(2, 1, 0, 3, 4)
        halves = halves.reshape(cores, *wg_shape)
        mine = lax.dynamic_index_in_dim(halves, core[0], 0, False)
        theirs = lax.dynamic_index_in_dim(halves, cores - 1 - core[0], 0, False).astype(BF)
        chip_wg = (mine + lax.ppermute(theirs, "cols", swap).astype(F32)).astype(BF)
    parts = lax.all_to_all(chip_wg, "rows", 0, 0, tiled=False)
    grad_left, grad_right, token = pl.pallas_call(
        functools.partial(finish_kernel, chips),
        out_shape=(shape(left_image.shape, BF),) * 2 + (shape((8, 128), F32),),
        in_specs=[SCALAR] * 2 + vmem(5),
        out_specs=vmem(3),
        scratch_shapes=[
            pltpu.VMEM((size + 2 * PAD, features), F32),
            pltpu.VMEM((band + 2 * PAD, features), F32),
        ],
        cost_estimate=LARGE,
        compiler_params=params(8),
    )(core, chip_at, whole_grad, taps, across_got, got_same, got_other)
    scale = 1.0 / math.sqrt(2 * depth * band * chips * cores)
    mine = pl.pallas_call(
        functools.partial(sum_kernel, scale),
        out_shape=shape(wg_shape[1:], F32),
        in_specs=vmem(2),
        out_specs=vmem(1)[0],
        cost_estimate=SMALL,
        compiler_params=params(4),
    )(parts, token)
    theirs = lax.ppermute(mine, "cols", swap)
    if tiled:
        weight_grad = pl.pallas_call(
            finish_weight_kernel,
            out_shape=shape((2 * piece, 9 * channels), F32),
            in_specs=[SCALAR] + vmem(2),
            out_specs=vmem(1)[0],
            cost_estimate=SMALL,
            compiler_params=params(4),
        )(core, mine, theirs)
    else:
        first = core[0] == 0
        both = jnp.stack([jnp.where(first, mine, theirs), jnp.where(first, theirs, mine)])
        both = both.reshape(cores, 3, piece, 3, channels).transpose(0, 2, 3, 1, 4)
        weight_grad = both.reshape(cores * piece, 9 * channels)
    return grad_left, grad_right, weight_grad


def solution(mesh):
    block = P(("pairs", "rows"), "cols", None)
    return jax.shard_map(
        on_device,
        mesh=mesh,
        in_specs=(block, block, P(), block, block, block, block),
        out_specs=(block, block, P(("pairs", "rows"), None)),
        check_vma=False,
    )
```

time: 73 us -> 43.8 us (0.60)
  the two profiles are of different devices: /device:TPU:21 before, /device:TPU:0 now
where the time goes in v2:
time: 43.8 us; the launch traced here: 43.5 us
  Pallas kernels  14.5 us (33%)
  waiting for transfers between devices  13.7 us (31%)
  starting transfers between devices  13.6 us (31%)
  local copies, waits for them, and re-layouts  0.86 us (2%)
  between operations  0.78 us (2%)
    all_to_all x1, waiting for transfers between devices, on_device(): parts = lax.all_to_all(chip_wg, 'rows', 0, 0, tiled=False)  8.35 us
    all_to_all x1, starting transfers between devices, on_device(): parts = lax.all_to_all(chip_wg, 'rows', 0, 0, tiled=False)  6.14 us
    pallas_call x1, Pallas kernels, on_device(): pl.pallas_call(functools.partial(main_kernel, chips), out_shape=(shape((2...  4.84 us
    ppermute x1, waiting for transfers between devices, on_device(): halo_same = lax.ppermute(near, flat, same_in)  3.62 us
    pallas_call x1, Pallas kernels, on_device(): pl.pallas_call(prepare_kernel, out_shape=(shape((2, size, features), F32)...  3.36 us
    ppermute x1, starting transfers between devices, on_device(): halo_other = lax.ppermute(own, flat, other)  2.59 us
    pallas_call x1, Pallas kernels, on_device(): pl.pallas_call(local_kernel, out_shape=(shape((band, reach), BF), shape((...  2.04 us
    pallas_call x1, Pallas kernels, on_device(): pl.pallas_call(functools.partial(finish_kernel, chips), out_shape=(shape(...  1.67 us
  transfers between devices with their start and end apart: 13, of which 4 were waited for; matrix products, arithmetic and copies ran while one was open for 0% of the time, Pallas kernels for 18%

profile of v2, /device:TPU:0, one launch (start us, length us, event | category | flops | bytes accessed | tf_op | source)
XLA Modules:
  0.0 43.5 jit_solution(10356167614409243643)
XLA Ops:
  0.6 1.1 %shard_map.94 = (bf16[2,512,128]{2,1,0:T(8,128)(2,1)S(1)}, bf16[2,512,128]{2,1,0:T(8,128)(2,1)S(1)}) custom-call(s32[1]{0:T(128)} %bitcast.core, bf16[2,512,128]{2,1,0:T(8,128)(2,1)} %left.3, bf16[2,512,128]{2,1,0:T(8,128)(2,1)} %right.3), custom_call_target="tpu_custom_call" | custom-call | flops 1 | bytes 1 | tf_op jit(solution)/shard_map/pallas_call | solution.py:380
  1.8 0.5 %collective-permute-start.2 = (bf16[2,512,128]{2,1,0:T(8,128)(2,1)}, bf16[2,512,128]{2,1,0:T(8,128)(2,1)S(1)}, u32[]{:S(2)}, u32[]{:S(2)}) collective-permute-start(bf16[2,512,128]{2,1,0:T(8,128)(2,1)} %left.3), channel_id=1, source_target_pairs={{0,1},{1,0},{2,3},{3,2},{4,5},{5,4},{6,7},{7,6},{8,9},{9,8},{10,11... | collective-permute-start | bytes 786440 | tf_op jit(solution)/shard_map/ppermute | solution.py:393
  2.3 0.1 collective-permute-start.6
  2.4 0.4 collective-permute-start.7
  2.8 2.6 %collective-permute-start.1 = (bf16[2,512,128]{2,1,0:T(8,128)(2,1)S(1)}, bf16[2,512,128]{2,1,0:T(8,128)(2,1)S(1)}, u32[]{:S(2)}, u32[]{:S(2)}) collective-permute-start(bf16[2,512,128]{2,1,0:T(8,128)(2,1)S(1)} %get-tuple-element.27), channel_id=1, source_target_pairs={{1,2},{2,1},{3,4},{4,3},{5,6},{6,5},{7,8},{8,7},{9,10},{10,9},{11,... | collective-permute-start | bytes 786440 | tf_op jit(solution)/shard_map/ppermute | solution.py:389
  5.4 0.1 collective-permute-start.3
  5.5 0.0 collective-permute-done.7.three_got
  5.5 0.0 copy-start.4
  5.5 0.4 collective-permute-start.5
  5.9 0.0 collective-permute-done.6.two_got
  5.9 0.0 copy-start.3
  5.9 1.2 %collective-permute-start = (bf16[2,512,128]{2,1,0:T(8,128)(2,1)S(1)}, bf16[2,512,128]{2,1,0:T(8,128)(2,1)S(1)}, u32[]{:S(2)}, u32[]{:S(2)}) collective-permute-start(bf16[2,512,128]{2,1,0:T(8,128)(2,1)S(1)} %get-tuple-element.26), channel_id=1, source_target_pairs={{0,2},{3,1},{2,4},{5,3},{4,6},{7,5},{6,8},{9,7},{8,10},{11,9},{10,... | collective-permute-start | bytes 786440 | tf_op jit(solution)/shard_map/ppermute | solution.py:390
  7.1 0.0 collective-permute-done.2.left_got
  7.1 0.0 copy-start.1
  7.1 0.0 collective-permute-start.4
  7.1 2.0 %shard_map.95 = (bf16[512,256]{1,0:T(8,128)(2,1)S(1)}, bf16[768,384]{1,0:T(8,128)(2,1)S(1)}, bf16[384,256]{1,0:T(8,128)(2,1)S(1)}) custom-call(s32[1]{0:T(128)} %bitcast.core, bf16[3,384,256]{2,1,0:T(8,128)(2,1)} %bitcast.5, bf16[2,512,256]{2,1,0:T(8,128)(2,1)} %zero_hbm.1, bf16[2,512,128]{2,1,0:T(8,128)(2,1)} %one_hbm.1, bf16[2,64,512]{2,1,0:T(8,128)(2,1)} %bitcast.8, ...), custom_call_target="tpu_custom_call" | custom-call | flops 99999997952 | bytes 1 | tf_op jit(solution)/shard_map/pallas_call | solution.py:397
  9.2 0.0 copy-done.4
  9.2 0.0 copy-done.3
  9.2 0.0 copy-done.1
  9.2 0.0 collective-permute-done.3.right_got
  9.2 0.0 copy-start.2
  9.2 0.0 collective-permute-done.5.one_got
  9.3 0.0 collective-permute-done.4.zero_got
  9.3 0.0 copy-start
  9.3 0.7 %copy-done.2 = bf16[2,512,128]{2,1,0:T(8,128)(2,1)} copy-done((bf16[2,512,128]{2,1,0:T(8,128)(2,1)}, bf16[2,512,128]{2,1,0:T(8,128)(2,1)S(1)}, u32[]{:S(2)}) %copy-start.2) | copy-done | bytes 262168
  9.9 0.2 copy-done
  10.1 3.4 %shard_map.96 = (f32[2,1024,256]{2,1,0:T(8,128)S(1)}, bf16[2,256,1024]{2,1,0:T(8,128)(2,1)S(1)}, bf16[4,256,512]{2,1,0:T(8,128)(2,1)S(1)}, bf16[4,512,256]{2,1,0:T(8,128)(2,1)S(1)}) custom-call(s32[1]{0:T(128)} %bitcast.core, bf16[2,512,128]{2,1,0:T(8,128)(2,1)} %left.3, bf16[2,512,128]{2,1,0:T(8,128)(2,1)} %right.3, bf16[2,512,128]{2,1,0:T(8,128)(2,1)} %copy-done.1, ...), custom_call_target="tpu_custom_call" | custom-call | flops 1 | bytes 1 | tf_op jit(solution)/shard_map/pallas_call | solution.py:417
  13.5 3.6 %collective-permute-done.halo_same = bf16[2,512,128]{2,1,0:T(8,128)(2,1)S(1)} collective-permute-done((bf16[2,512,128]{2,1,0:T(8,128)(2,1)S(1)}, bf16[2,512,128]{2,1,0:T(8,128)(2,1)S(1)}, u32[]{:S(2)}, u32[]{:S(2)}) %collective-permute-start) | collective-permute-done | bytes 262176 | tf_op jit(solution)/shard_map/ppermute | solution.py:390
  17.1 0.0 collective-permute-done.1.halo_other
  17.1 4.8 %shard_map.97 = (bf16[2,1024,256]{2,1,0:T(8,128)(2,1)S(1)}, bf16[2,512,128]{2,1,0:T(8,128)(2,1)}, bf16[2,512,128]{2,1,0:T(8,128)(2,1)}, f32[8,48,384]{2,1,0:T(8,128)S(1)}, bf16[7,512,128]{2,1,0:T(8,128)(2,1)S(1)}) custom-call(s32[1]{0:T(128)} %bitcast.core, s32[1]{0:T(128)} %bitcast.1.chip, bf16[2,512,128]{2,1,0:T(8,128)(2,1)S(1)} %collective-permute-done.halo_same, ...), custom_call_target="tpu_custom_call" | custom-call | flops 1 | bytes 1 | tf_op jit(solution)/shard_map/pallas_call | solution.py:447
  22.0 0.1 collective-permute-start.8
  22.0 0.5 %collective-permute-start.9 = (bf16[2,512,128]{2,1,0:T(8,128)(2,1)}, bf16[2,512,128]{2,1,0:T(8,128)(2,1)S(1)}, u32[]{:S(2)}, u32[]{:S(2)}) collective-permute-start(bf16[2,512,128]{2,1,0:T(8,128)(2,1)} %get-tuple-element.43), channel_id=1, source_target_pairs={{2,0},{1,3},{4,2},{3,5},{6,4},{5,7},{8,6},{7,9},{10,8},{9,11},{12,... | collective-permute-start | bytes 786440 | tf_op jit(solution)/shard_map/ppermute | solution.py:473
  22.5 1.5 %collective-permute-start.10 = (bf16[2,512,128]{2,1,0:T(8,128)(2,1)}, bf16[2,512,128]{2,1,0:T(8,128)(2,1)S(1)}, u32[]{:S(2)}, u32[]{:S(2)}) collective-permute-start(bf16[2,512,128]{2,1,0:T(8,128)(2,1)} %get-tuple-element.44), channel_id=1, source_target_pairs={{1,2},{2,1},{3,4},{4,3},{5,6},{6,5},{7,8},{8,7},{9,10},{10,9},{11,... | collective-permute-start | bytes 786440 | tf_op jit(solution)/shard_map/ppermute | solution.py:472
  24.1 0.4 %collective-permute-done.8.across = bf16[7,512,128]{2,1,0:T(8,128)(2,1)S(1)} collective-permute-done((bf16[7,512,128]{2,1,0:T(8,128)(2,1)S(1)}, bf16[7,512,128]{2,1,0:T(8,128)(2,1)S(1)}, u32[]{:S(2)}, u32[]{:S(2)}) %collective-permute-start.8) | collective-permute-done | bytes 917536 | tf_op jit(solution)/shard_map/ppermute | solution.py:474
  24.5 0.8 %shard_map.99 = bf16[8,48,384]{2,1,0:T(8,128)(2,1)} custom-call(f32[8,48,384]{2,1,0:T(8,128)S(1)} %get-tuple-element.47.keep, bf16[7,512,128]{2,1,0:T(8,128)(2,1)S(1)} %collective-permute-done.8.across), custom_call_target="tpu_custom_call" | custom-call | flops 1 | bytes 1 | tf_op jit(solution)/shard_map/pallas_call | solution.py:476
  25.3 6.1 %all-to-all-start = ((bf16[8,48,384]{2,1,0:T(8,128)(2,1)}), bf16[8,48,384]{2,1,0:T(8,128)(2,1)S(1)}, u32[]{:S(2)}, u32[]{:S(2)}) async-start(bf16[8,48,384]{2,1,0:T(8,128)(2,1)} %shard_map.99), calls=%async_computation | async-start | bytes 589824 | tf_op jit(solution)/shard_map/all_to_all | solution.py:490
  31.4 0.0 collective-permute-done.9.edge_same
  31.4 0.0 collective-permute-done.10.edge_other
  31.4 1.7 %shard_map.98 = (bf16[2,512,128]{2,1,0:T(8,128)(2,1)}, bf16[2,512,128]{2,1,0:T(8,128)(2,1)}, f32[8,128]{1,0:T(8,128)S(1)}) custom-call(s32[1]{0:T(128)} %bitcast.core, s32[1]{0:T(128)} %bitcast.1.chip, bf16[2,1024,256]{2,1,0:T(8,128)(2,1)S(1)} %get-tuple-element.41.whole_grad, bf16[768,384]{1,0:T(8,128)(2,1)S(1)} %get-tuple-element.40.taps, ...), custom_call_target="tpu_custom_call" | custom-call | flops 99999997952 | bytes 1 | tf_op jit(solution)/shard_map/pallas_call | solution.py:491
  33.1 8.3 %all-to-all-done.parts = bf16[8,48,384]{2,1,0:T(8,128)(2,1)S(1)} async-done(((bf16[8,48,384]{2,1,0:T(8,128)(2,1)}), bf16[8,48,384]{2,1,0:T(8,128)(2,1)S(1)}, u32[]{:S(2)}, u32[]{:S(2)}) %all-to-all-start) | async-done | bytes 294944 | tf_op jit(solution)/shard_map/all_to_all | solution.py:490
  41.5 0.1 collective-permute-start.11
  41.6 1.3 %collective-permute-done.11.got = f32[48,384]{1,0:T(8,128)S(1)} collective-permute-done((f32[48,384]{1,0:T(8,128)S(1)}, f32[48,384]{1,0:T(8,128)S(1)}, u32[]{:S(2)}, u32[]{:S(2)}) %collective-permute-start.11) | collective-permute-done | bytes 73760 | tf_op jit(solution)/shard_map/ppermute | solution.py:512
  42.8 0.7 %shard_map.101 = f32[32,1152]{1,0:T(8,128)} custom-call(s32[1]{0:T(128)} %bitcast.core, f32[48,384]{1,0:T(8,128)S(1)} %shard_map.100.mine, f32[48,384]{1,0:T(8,128)S(1)} %collective-permute-done.11.got), custom_call_target="tpu_custom_call" | custom-call | flops 1 | bytes 1 | tf_op jit(solution)/shard_map/pallas_call | solution.py:514
  (1 shorter events, 0.0 us)
Async XLA Ops:
  1.8 5.4 %collective-permute-start.2 = (bf16[2,512,128]{2,1,0:T(8,128)(2,1)}, bf16[2,512,128]{2,1,0:T(8,128)(2,1)S(1)}, u32[]{:S(2)}, u32[]{:S(2)}) collective-permute-start(bf16[2,512,128]{2,1,0:T(8,128)(2,1)} %left.3), channel_id=1, source_target_pairs={{0,1},{1,0},{2,3},{3,2},{4,5},{5,4},{6,7},{7,6},{8,9},{9,8},{10,11... | collective-permute-start | bytes 786440 | tf_op jit(solution)/shard_map/ppermute | solution.py:393
  2.3 3.6 %collective-permute-start.6 = (bf16[2,64,512]{2,1,0:T(8,128)(2,1)}, bf16[2,64,512]{2,1,0:T(8,128)(2,1)S(1)}, u32[]{:S(2)}, u32[]{:S(2)}) collective-permute-start(bf16[2,64,512]{2,1,0:T(8,128)(2,1)} %bitcast.7), channel_id=1, source_target_pairs={{0,1},{1,0},{2,3},{3,2},{4,5},{5,4},{6,7},{7,6},{8,9},{9,8},{10,11... | collective-permute-start | bytes 393224 | tf_op jit(solution)/shard_map/ppermute | solution.py:393
  2.4 3.1 %collective-permute-start.7 = (bf16[2,32,512]{2,1,0:T(8,128)(2,1)}, bf16[2,32,512]{2,1,0:T(8,128)(2,1)S(1)}, u32[]{:S(2)}, u32[]{:S(2)}) collective-permute-start(bf16[2,32,512]{2,1,0:T(8,128)(2,1)} %bitcast.9), channel_id=1, source_target_pairs={{0,1},{1,0},{2,3},{3,2},{4,5},{5,4},{6,7},{7,6},{8,9},{9,8},{10,11... | collective-permute-start | bytes 196616 | tf_op jit(solution)/shard_map/ppermute | solution.py:393
  2.8 14.3 %collective-permute-start.1 = (bf16[2,512,128]{2,1,0:T(8,128)(2,1)S(1)}, bf16[2,512,128]{2,1,0:T(8,128)(2,1)S(1)}, u32[]{:S(2)}, u32[]{:S(2)}) collective-permute-start(bf16[2,512,128]{2,1,0:T(8,128)(2,1)S(1)} %get-tuple-element.27), channel_id=1, source_target_pairs={{1,2},{2,1},{3,4},{4,3},{5,6},{6,5},{7,8},{8,7},{9,10},{10,9},{11,... | collective-permute-start | bytes 786440 | tf_op jit(solution)/shard_map/ppermute | solution.py:389
  5.4 3.8 %collective-permute-start.3 = (bf16[2,512,128]{2,1,0:T(8,128)(2,1)}, bf16[2,512,128]{2,1,0:T(8,128)(2,1)S(1)}, u32[]{:S(2)}, u32[]{:S(2)}) collective-permute-start(bf16[2,512,128]{2,1,0:T(8,128)(2,1)} %right.3), channel_id=1, source_target_pairs={{0,1},{1,0},{2,3},{3,2},{4,5},{5,4},{6,7},{7,6},{8,9},{9,8},{10,11... | collective-permute-start | bytes 786440 | tf_op jit(solution)/shard_map/ppermute | solution.py:393
  5.5 3.7 %copy-start.4 = (bf16[2,32,512]{2,1,0:T(8,128)(2,1)}, bf16[2,32,512]{2,1,0:T(8,128)(2,1)S(1)}, u32[]{:S(2)}) copy-start(bf16[2,32,512]{2,1,0:T(8,128)(2,1)S(1)} %collective-permute-done.7.three_got) | copy-start | bytes 196612
  5.5 3.8 %collective-permute-start.5 = (bf16[2,512,128]{2,1,0:T(8,128)(2,1)}, bf16[2,512,128]{2,1,0:T(8,128)(2,1)}, u32[]{:S(2)}, u32[]{:S(2)}) collective-permute-start(bf16[2,512,128]{2,1,0:T(8,128)(2,1)} %one_hbm.1), channel_id=1, source_target_pairs={{0,1},{1,0},{2,3},{3,2},{4,5},{5,4},{6,7},{7,6},{8,9},{9,8},{10,11... | collective-permute-start | bytes 786440 | tf_op jit(solution)/shard_map/ppermute | solution.py:393
  5.9 3.3 %copy-start.3 = (bf16[2,64,512]{2,1,0:T(8,128)(2,1)}, bf16[2,64,512]{2,1,0:T(8,128)(2,1)S(1)}, u32[]{:S(2)}) copy-start(bf16[2,64,512]{2,1,0:T(8,128)(2,1)S(1)} %collective-permute-done.6.two_got) | copy-start | bytes 393220
  5.9 11.2 %collective-permute-start = (bf16[2,512,128]{2,1,0:T(8,128)(2,1)S(1)}, bf16[2,512,128]{2,1,0:T(8,128)(2,1)S(1)}, u32[]{:S(2)}, u32[]{:S(2)}) collective-permute-start(bf16[2,512,128]{2,1,0:T(8,128)(2,1)S(1)} %get-tuple-element.26), channel_id=1, source_target_pairs={{0,2},{3,1},{2,4},{5,3},{4,6},{7,5},{6,8},{9,7},{8,10},{11,9},{10,... | collective-permute-start | bytes 786440 | tf_op jit(solution)/shard_map/ppermute | solution.py:390
  7.1 2.1 %copy-start.1 = (bf16[2,512,128]{2,1,0:T(8,128)(2,1)}, bf16[2,512,128]{2,1,0:T(8,128)(2,1)S(1)}, u32[]{:S(2)}) copy-start(bf16[2,512,128]{2,1,0:T(8,128)(2,1)S(1)} %collective-permute-done.2.left_got) | copy-start | bytes 786436
  7.1 2.1 %collective-permute-start.4 = (bf16[2,512,256]{2,1,0:T(8,128)(2,1)}, bf16[2,512,256]{2,1,0:T(8,128)(2,1)S(1)}, u32[]{:S(2)}, u32[]{:S(2)}) collective-permute-start(bf16[2,512,256]{2,1,0:T(8,128)(2,1)} %zero_hbm.1), channel_id=1, source_target_pairs={{0,1},{1,0},{2,3},{3,2},{4,5},{5,4},{6,7},{7,6},{8,9},{9,8},{10,11... | collective-permute-start | bytes 1572872 | tf_op jit(solution)/shard_map/ppermute | solution.py:393
  9.2 0.7 %copy-start.2 = (bf16[2,512,128]{2,1,0:T(8,128)(2,1)}, bf16[2,512,128]{2,1,0:T(8,128)(2,1)S(1)}, u32[]{:S(2)}) copy-start(bf16[2,512,128]{2,1,0:T(8,128)(2,1)S(1)} %collective-permute-done.3.right_got) | copy-start | bytes 786436
  9.3 0.9 %copy-start = (bf16[2,512,256]{2,1,0:T(8,128)(2,1)}, bf16[2,512,256]{2,1,0:T(8,128)(2,1)S(1)}, u32[]{:S(2)}) copy-start(bf16[2,512,256]{2,1,0:T(8,128)(2,1)S(1)} %collective-permute-done.4.zero_got) | copy-start | bytes 1572868
  22.0 2.5 %collective-permute-start.8 = (bf16[7,512,128]{2,1,0:T(8,128)(2,1)S(1)}, bf16[7,512,128]{2,1,0:T(8,128)(2,1)S(1)}, u32[]{:S(2)}, u32[]{:S(2)}) collective-permute-start(bf16[7,512,128]{2,1,0:T(8,128)(2,1)S(1)} %get-tuple-element.42), channel_id=1, source_target_pairs={{0,1},{1,0},{2,3},{3,2},{4,5},{5,4},{6,7},{7,6},{8,9},{9,8},{10,11... | collective-permute-start | bytes 2752520 | tf_op jit(solution)/shard_map/ppermute | solution.py:474
  22.0 9.4 %collective-permute-start.9 = (bf16[2,512,128]{2,1,0:T(8,128)(2,1)}, bf16[2,512,128]{2,1,0:T(8,128)(2,1)S(1)}, u32[]{:S(2)}, u32[]{:S(2)}) collective-permute-start(bf16[2,512,128]{2,1,0:T(8,128)(2,1)} %get-tuple-element.43), channel_id=1, source_target_pairs={{2,0},{1,3},{4,2},{3,5},{6,4},{5,7},{8,6},{7,9},{10,8},{9,11},{12,... | collective-permute-start | bytes 786440 | tf_op jit(solution)/shard_map/ppermute | solution.py:473
  22.5 8.9 %collective-permute-start.10 = (bf16[2,512,128]{2,1,0:T(8,128)(2,1)}, bf16[2,512,128]{2,1,0:T(8,128)(2,1)S(1)}, u32[]{:S(2)}, u32[]{:S(2)}) collective-permute-start(bf16[2,512,128]{2,1,0:T(8,128)(2,1)} %get-tuple-element.44), channel_id=1, source_target_pairs={{1,2},{2,1},{3,4},{4,3},{5,6},{6,5},{7,8},{8,7},{9,10},{10,9},{11,... | collective-permute-start | bytes 786440 | tf_op jit(solution)/shard_map/ppermute | solution.py:472
  25.3 16.2 %all-to-all-start = ((bf16[8,48,384]{2,1,0:T(8,128)(2,1)}), bf16[8,48,384]{2,1,0:T(8,128)(2,1)S(1)}, u32[]{:S(2)}, u32[]{:S(2)}) async-start(bf16[8,48,384]{2,1,0:T(8,128)(2,1)} %shard_map.99), calls=%async_computation | async-start | bytes 589824 | tf_op jit(solution)/shard_map/all_to_all | solution.py:490
  41.5 1.3 %collective-permute-start.11 = (f32[48,384]{1,0:T(8,128)S(1)}, f32[48,384]{1,0:T(8,128)S(1)}, u32[]{:S(2)}, u32[]{:S(2)}) collective-permute-start(f32[48,384]{1,0:T(8,128)S(1)} %shard_map.100.mine), channel_id=1, source_target_pairs={{0,1},{1,0},{2,3},{3,2},{4,5},{5,4},{6,7},{7,6},{8,9},{9,8},{10,11... | collective-permute-start | bytes 221192 | tf_op jit(solution)/shard_map/ppermute | solution.py:512

commit v3 on v2

--- a/solution.py
+++ b/solution.py
@@ -39,17 +39,48 @@
     return pltpu.CompilerParams(vmem_limit_bytes=mib * MIB)
 
 
-def first_kernel(core, left, right, own, near, sems):
-    c = core[0]
-    copies = []
-    for target, row in ((own, c), (near, 1 - c)):
-        for image, source in enumerate((left, right)):
-            copies.append(
-                pltpu.make_async_copy(source.at[row], target.at[image], sems.at[len(copies)])
-            )
+def started(moves, sems):
+    copies = [
+        pltpu.make_async_copy(source, target, sems.at[index])
+        for index, (source, target) in enumerate(moves)
+    ]
     for copy in copies:
         copy.start()
-    for copy in copies:
+    return copies
+
+
+def packed(source, target, first):
+    count, lanes = source.shape[0], target.shape[1]
+    moves = []
+    for index in range(source.shape[1] // lanes):
+        moves.append(
+            (source.at[:, pl.ds(index * lanes, lanes)], target.at[pl.ds(first, count)])
+        )
+        first += count
+    return moves, first
+
+
+def level_moves(levels, pack, first):
+    moves = []
+    for level in levels:
+        more, first = packed(level, pack, first)
+        moves += more
+    return moves
+
+
+def first_kernel(
+    core, left, right, zero, one, two, three,
+    own, near, pack, sems,
+):
+    c = core[0]
+    half = left.shape[1]
+    moves = []
+    for image, source in enumerate((left, right)):
+        moves += [(source.at[c], own.at[image]), (source.at[1 - c], near.at[image])]
+    for index, source in enumerate((left.at[c], left.at[1 - c], right.at[c], right.at[1 - c])):
+        moves.append((source, pack.at[pl.ds(index * half, half)]))
+    moves += level_moves([x.at[1 - c] for x in (zero, one, two, three)], pack, 4 * half)
+    for copy in started(moves, sems):
         copy.wait()
 
 
@@ -73,9 +104,9 @@
     return dot(total.astype(BF), mirror).astype(BF)
 
 
-def shifted_3(scratch, size):
+def shifted_3(scratch, size, first=0):
     return jnp.concatenate(
-        [scratch[pl.ds(PAD + by, size)].astype(BF) for by in (-1, 0, 1)], axis=1
+        [scratch[pl.ds(PAD + first + by, size)].astype(BF) for by in (-1, 0, 1)], axis=1
     )
 
 
@@ -85,19 +116,9 @@
     scratch[pl.ds(PAD + size, PAD)] = zeros
 
 
-def started(moves, sems):
-    copies = [
-        pltpu.make_async_copy(source, target, sems.at[index])
-        for index, (source, target) in enumerate(moves)
-    ]
-    for copy in copies:
-        copy.start()
-    return copies
-
-
 def local_kernel(
     core, weight_hbm, zero_hbm, one_hbm, two_hbm, three_hbm,
-    corr, taps, outer_weight,
+    corr, taps,
     weight, zero, one, two, three, sems,
 ):
     c = core[0]
@@ -120,16 +141,14 @@
             taps[pl.ds(col * features, features), pl.ds(place * channels, channels)] = (
                 piece.T.astype(BF)
             )
-    outer_weight[...] = weight[2 * c]
     for copy in copies[1:]:
         copy.wait()
     corr[...] = mirrored(zero[...], one[...], two[...], three[...])
 
 
 def prepare_kernel(
-    core, left, right, left_got, right_got, zero_got, one_got, two_got, three_got, weight_hbm,
-    corr,
-    own_sum, images_t, band, band_t,
+    core, left, right, got, weight_hbm, corr,
+    own_sum, images_t, band, band_t, outer_weight,
     padded, rows, images, weight, zero, one, two, three, sems,
 ):
     c = core[0]
@@ -139,24 +158,23 @@
     reach = corr.shape[1]
     here = pl.multiple_of(c * half, half)
     there = pl.multiple_of((1 - c) * half, half)
-    moves = [
-        (zero_got.at[c], zero),
-        (one_got.at[c], one),
-        (two_got.at[c], two),
-        (three_got.at[c], three),
-    ]
-    for image, (mine, got) in enumerate(((left, left_got), (right, right_got))):
+    moves = [(b, a) for a, b in level_moves((zero, one, two, three), got, 4 * half)]
+    levels = len(moves)
+    for image, mine in enumerate((left, right)):
         for role, row in enumerate((c, 1 - c)):
+            block = 2 * image + 1 - role
             moves.append((mine.at[row], images.at[image, role, pl.ds(here, half)]))
-            moves.append((got.at[row], images.at[image, role, pl.ds(there, half)]))
+            moves.append(
+                (got.at[pl.ds(block * half, half)], images.at[image, role, pl.ds(there, half)])
+            )
     moves.append((weight_hbm, weight))
     copies = started(moves, sems)
     clear_pads(padded, size)
     rows[pl.ds(here, half)] = corr[...]
-    for copy in copies[:4]:
+    for copy in copies[:levels]:
         copy.wait()
     rows[pl.ds(there, half)] = mirrored(zero[...], one[...], two[...], three[...])
-    for copy in copies[4:]:
+    for copy in copies[levels:]:
         copy.wait()
     for image in range(2):
         total = None
@@ -167,6 +185,7 @@
             part = dot(shifted_3(padded, size), weight[tap])
             total = part if total is None else total + part
         own_sum[image] = total
+    outer_weight[...] = weight[2 * c]
     for block in range(size // reach):
         values = rows[pl.ds(block * reach, reach)].astype(F32)
         wide = jnp.concatenate([values, jnp.zeros_like(values)], axis=1)
@@ -182,7 +201,7 @@
 def main_kernel(
     chips, core, chip, halo_same, halo_other, weight, own_sum, images_t, band, band_t, taps,
     whole_grad, edge_same, edge_other, wg_keep, across,
-    padded, feats, wide, grads, wg, edges, pair, edge_sems,
+    padded, feats, wide, grads, wg, edges, edge_sems,
 ):
     c = core[0]
     half = halo_same.shape[1]
@@ -201,9 +220,10 @@
         for place, halo in ((here, halo_same), (there, halo_other)):
             padded[pl.ds(PAD + place, half)] = jnp.where(alone, 0.0, halo[image].astype(F32))
         halo_t.append(padded[pl.ds(PAD, size)].T.astype(BF))
-        feats[image] = (
-            own_sum[image] + dot(shifted_3(padded, size), weight[...])
-        ).astype(BF)
+        for block in range(blocks):
+            rows = pl.ds(block * reach, reach)
+            part = dot(shifted_3(padded, reach, block * reach), weight[...])
+            feats[image, rows] = (own_sum[image, rows] + part).astype(BF)
     for image in range(2):
         for block in range(blocks):
             low = pl.ds(block * reach, reach)
@@ -232,13 +252,8 @@
             pltpu.make_async_copy(
                 edges.at[index, image], out.at[image], edge_sems.at[2 * image + index]
             ).start()
-    inner = None
-    outer = None
-    for image in range(2):
-        part = dot(images_t[image], grads[image])
-        inner = part if inner is None else inner + part
-        part = dot(halo_t[image], grads[image])
-        outer = part if outer is None else outer + part
+    inner = dot(images_t[0], grads[0]) + dot(images_t[1], grads[1])
+    outer = dot(halo_t[0], grads[0]) + dot(halo_t[1], grads[1])
     for image in range(2):
         for index, out in enumerate((edge_same, edge_other)):
             pltpu.make_async_copy(
@@ -252,10 +267,9 @@
     wg[:, pl.ds(channels, channels)] = own_wg
     wg[:, pl.ds(2 * channels, channels)] = jnp.where(first, inner_wg, outer_wg)
     for image in range(2):
-        pair[...] = dot(grads[image], taps[:, pl.ds(channels, 2 * channels)])
+        pair = dot(grads[image, pl.ds(there, half)], taps[:, pl.ds(channels, 2 * channels)])
         for role, row in ((0, c), (1, 1 - c)):
-            lanes = pl.ds(role * channels, channels)
-            across[2 * image + row] = pair[pl.ds(there, half), lanes].astype(BF)
+            across[2 * image + row] = pair[:, role * channels : (role + 1) * channels].astype(BF)
     if wg_keep.shape == wg.shape:
         wg_keep[...] = wg[...]
         return
@@ -377,32 +391,29 @@
     )
     in_hbm = [pltpu.with_memory_space_constraint(x, pltpu.HBM) for x in params_in]
     any_space = pl.BlockSpec(memory_space=pl.ANY)
-    own, near = pl.pallas_call(
+    level_rows = band * (reach + reach // 2 + reach // 4 + reach // 8) // channels
+    level_copies = (reach + reach // 2) // channels + 2 * (band // channels)
+    own, near, pack = pl.pallas_call(
         first_kernel,
-        out_shape=(row_shape, row_shape),
-        in_specs=[SCALAR] + [any_space] * 2,
-        out_specs=vmem(2),
-        scratch_shapes=[pltpu.SemaphoreType.DMA((4,))],
+        out_shape=(row_shape,) * 2 + (shape((4 * band + level_rows, channels), BF),),
+        in_specs=[SCALAR] + [any_space] * 6,
+        out_specs=vmem(3),
+        scratch_shapes=[pltpu.SemaphoreType.DMA((8 + level_copies,))],
         cost_estimate=SMALL,
         compiler_params=params(2),
-    )(core, *in_hbm[:2])
+    )(core, *in_hbm[:6])
     halo_other = lax.ppermute(own, flat, other)
     halo_same = lax.ppermute(near, flat, same_in)
-    from_core = lax.optimization_barrier((own, *params_in))[1:]
-    got = [
-        pltpu.with_memory_space_constraint(lax.ppermute(x, "cols", swap), pltpu.HBM)
-        for x in from_core[:6]
-    ]
-
-    corr, taps, outer_weight = pl.pallas_call(
+    got = pltpu.with_memory_space_constraint(lax.ppermute(pack, "cols", swap), pltpu.HBM)
+
+    corr, taps = pl.pallas_call(
         local_kernel,
         out_shape=(
             shape((band, reach), BF),
             shape((3 * features, 3 * channels), BF),
-            shape((3 * channels, features), BF),
         ),
         in_specs=[SCALAR] + [any_space] * 5,
-        out_specs=vmem(3),
+        out_specs=vmem(2),
         scratch_shapes=[
             pltpu.VMEM((3, 3 * channels, features), BF),
             pltpu.VMEM((band, reach), BF),
@@ -414,16 +425,17 @@
         cost_estimate=LARGE,
         compiler_params=params(8),
     )(core, in_hbm[6], *in_hbm[2:6])
-    own_sum, images_t, skew, skew_t = pl.pallas_call(
+    own_sum, images_t, skew, skew_t, outer_weight = pl.pallas_call(
         prepare_kernel,
         out_shape=(
             shape((2, size, features), F32),
             shape((2, 2 * channels, size), BF),
             shape((blocks, reach, 2 * reach), BF),
             shape((blocks, 2 * reach, reach), BF),
+            shape((3 * channels, features), BF),
         ),
-        in_specs=[SCALAR] + [any_space] * 9 + vmem(1),
-        out_specs=vmem(4),
+        in_specs=[SCALAR] + [any_space] * 4 + vmem(1),
+        out_specs=vmem(5),
         scratch_shapes=[
             pltpu.VMEM((size + 2 * PAD, channels), F32),
             pltpu.VMEM((size, reach), BF),
@@ -433,11 +445,11 @@
             pltpu.VMEM((band, reach // 2), BF),
             pltpu.VMEM((reach // 4, band), BF),
             pltpu.VMEM((reach // 8, band), BF),
-            pltpu.SemaphoreType.DMA((13,)),
+            pltpu.SemaphoreType.DMA((9 + level_copies,)),
         ],
         cost_estimate=SMALL,
         compiler_params=params(12),
-    )(core, *in_hbm[:2], *got, in_hbm[6], corr)
+    )(core, *in_hbm[:2], got, in_hbm[6], corr)
 
     piece = features // chips // cores
     tiled = piece % 16 == 0
@@ -462,7 +474,6 @@
             pltpu.VMEM((2, size, 3 * features), BF),
             pltpu.VMEM((3 * features, 3 * channels), F32),
             pltpu.VMEM((2, *row_shape.shape), BF),
-            pltpu.VMEM((size, 2 * channels), F32),
             pltpu.SemaphoreType.DMA((4,)),
         ],
         cost_estimate=SMALL,

time: 43.8 us -> 43.5 us (level)
  waiting for transfers between devices: 13.7 us -> 15.2 us
  starting transfers between devices: 13.6 us -> 12.7 us
  local copies, waits for them, and re-layouts: 0.86 us -> 0 us
    ppermute x1, starting transfers between devices: 1.2 us -> 3 us  [on_device(): halo_same = lax.ppermute(near, flat, same_in)]
    ppermute x6 -> x1, starting transfers between devices: 1.54 us -> 0.14 us  [on_device(): lax.ppermute(pack, 'cols', swap)]
    ppermute x1, starting transfers between devices: 2.59 us -> 1.52 us  [on_device(): halo_other = lax.ppermute(own, flat, other)]
    unnamed x10 -> x0, local copies, waits for them, and re-layouts: 0.86 us -> none
    ppermute x6 -> x1, waiting for transfers between devices: 0.02 us -> 0.65 us  [on_device(): lax.ppermute(pack, 'cols', swap)]
    ppermute x1, waiting for transfers between devices: 3.62 us -> 4.17 us  [on_device(): halo_same = lax.ppermute(near, flat, same_in)]
    pallas_call x1, Pallas kernels: 4.84 us -> 4.3 us  [on_device(): pl.pallas_call(functools.partial(main_kernel, chips), out_shape=(shape((2...]
    pallas_call x1, Pallas kernels: 1.13 us -> 1.59 us  [on_device(): pl.pallas_call(first_kernel, out_shape=(row_shape,) * 2 + (shape((4 * ban...]
  transfers between devices with their start and end apart: 13 -> 8, of which waited for: 4 -> 5; matrix products, arithmetic and copies ran while one was open for 0% -> 0% of each run, Pallas kernels for 18% -> 18%
where the time goes in v3:
time: 43.5 us; the launch traced here: 43.2 us
  waiting for transfers between devices  15.2 us (35%)
  Pallas kernels  14.5 us (33%)
  starting transfers between devices  12.7 us (29%)
  between operations  0.7 us (2%)
    all_to_all x1, waiting for transfers between devices, on_device(): parts = lax.all_to_all(chip_wg, 'rows', 0, 0, tiled=False)  8.69 us
    all_to_all x1, starting transfers between devices, on_device(): parts = lax.all_to_all(chip_wg, 'rows', 0, 0, tiled=False)  5.87 us
    pallas_call x1, Pallas kernels, on_device(): pl.pallas_call(functools.partial(main_kernel, chips), out_shape=(shape((2...  4.3 us
    ppermute x1, waiting for transfers between devices, on_device(): halo_same = lax.ppermute(near, flat, same_in)  4.17 us
    pallas_call x1, Pallas kernels, on_device(): pl.pallas_call(prepare_kernel, out_shape=(shape((2, size, features), F32)...  3.54 us
    ppermute x1, starting transfers between devices, on_device(): halo_same = lax.ppermute(near, flat, same_in)  3 us
    pallas_call x1, Pallas kernels, on_device(): pl.pallas_call(local_kernel, out_shape=(shape((band, reach), BF), shape((...  1.94 us
    pallas_call x1, Pallas kernels, on_device(): pl.pallas_call(functools.partial(finish_kernel, chips), out_shape=(shape(...  1.67 us
  transfers between devices with their start and end apart: 8, of which 5 were waited for; matrix products, arithmetic and copies ran while one was open for 0% of the time, Pallas kernels for 18%

profile of v3, /device:TPU:0, one launch (start us, length us, event | category | flops | bytes accessed | tf_op | source)
XLA Modules:
  0.0 43.2 jit_solution(8231419633425609324)
XLA Ops:
  0.6 1.6 %shard_map.94 = (bf16[2,512,128]{2,1,0:T(8,128)(2,1)S(1)}, bf16[2,512,128]{2,1,0:T(8,128)(2,1)S(1)}, bf16[3968,128]{1,0:T(8,128)(2,1)S(1)}) custom-call(s32[1]{0:T(128)} %bitcast.core, bf16[2,512,128]{2,1,0:T(8,128)(2,1)} %left.3, bf16[2,512,128]{2,1,0:T(8,128)(2,1)} %right.3, bf16[2,512,256]{2,1,0:T(8,128)(2,1)} %zero_hbm.1, bf16[2,512,128]{2,1,0:T(8,128)(2,1)} %one_hbm.1, ...), custom_call_target="tpu_custom_call" | custom-call | flops 1 | bytes 1 | tf_op jit(solution)/shard_map/pallas_call | solution.py:396
  2.2 3.0 %collective-permute-start = (bf16[2,512,128]{2,1,0:T(8,128)(2,1)S(1)}, bf16[2,512,128]{2,1,0:T(8,128)(2,1)S(1)}, u32[]{:S(2)}, u32[]{:S(2)}) collective-permute-start(bf16[2,512,128]{2,1,0:T(8,128)(2,1)S(1)} %get-tuple-element.21), channel_id=1, source_target_pairs={{0,2},{3,1},{2,4},{5,3},{4,6},{7,5},{6,8},{9,7},{8,10},{11,9},{10,... | collective-permute-start | bytes 786440 | tf_op jit(solution)/shard_map/ppermute | solution.py:406
  5.2 1.5 %collective-permute-start.1 = (bf16[2,512,128]{2,1,0:T(8,128)(2,1)S(1)}, bf16[2,512,128]{2,1,0:T(8,128)(2,1)S(1)}, u32[]{:S(2)}, u32[]{:S(2)}) collective-permute-start(bf16[2,512,128]{2,1,0:T(8,128)(2,1)S(1)} %get-tuple-element.22), channel_id=1, source_target_pairs={{1,2},{2,1},{3,4},{4,3},{5,6},{6,5},{7,8},{8,7},{9,10},{10,9},{11,... | collective-permute-start | bytes 786440 | tf_op jit(solution)/shard_map/ppermute | solution.py:405
  6.7 0.1 collective-permute-start.2
  6.9 1.9 %shard_map.95 = (bf16[512,256]{1,0:T(8,128)(2,1)S(1)}, bf16[768,384]{1,0:T(8,128)(2,1)S(1)}) custom-call(s32[1]{0:T(128)} %bitcast.core, bf16[3,384,256]{2,1,0:T(8,128)(2,1)} %bitcast.5, bf16[2,512,256]{2,1,0:T(8,128)(2,1)} %zero_hbm.1, bf16[2,512,128]{2,1,0:T(8,128)(2,1)} %one_hbm.1, bf16[2,64,512]{2,1,0:T(8,128)(2,1)} %bitcast.8, bf16[2,32,512]{2,1,0:T(8,128)(2,1)} %bitcast.10), custom_call_target="tpu_custom_call" | custom-call | flops 99999997952 | bytes 1 | tf_op jit(solution)/shard_map/pallas_call | solution.py:409
  8.8 0.7 %collective-permute-done.2.got = bf16[3968,128]{1,0:T(8,128)(2,1)} collective-permute-done((bf16[3968,128]{1,0:T(8,128)(2,1)S(1)}, bf16[3968,128]{1,0:T(8,128)(2,1)}, u32[]{:S(2)}, u32[]{:S(2)}) %collective-permute-start.2) | collective-permute-done | bytes 1015840 | tf_op jit(solution)/shard_map/ppermute | solution.py:407
  9.5 3.5 %shard_map.96 = (f32[2,1024,256]{2,1,0:T(8,128)S(1)}, bf16[2,256,1024]{2,1,0:T(8,128)(2,1)S(1)}, bf16[4,256,512]{2,1,0:T(8,128)(2,1)S(1)}, bf16[4,512,256]{2,1,0:T(8,128)(2,1)S(1)}, bf16[384,256]{1,0:T(8,128)(2,1)S(1)}) custom-call(s32[1]{0:T(128)} %bitcast.core, bf16[2,512,128]{2,1,0:T(8,128)(2,1)} %left.3, bf16[2,512,128]{2,1,0:T(8,128)(2,1)} %right.3, ...), custom_call_target="tpu_custom_call" | custom-call | flops 1 | bytes 1 | tf_op jit(solution)/shard_map/pallas_call | solution.py:428
  13.0 4.2 %collective-permute-done.halo_same = bf16[2,512,128]{2,1,0:T(8,128)(2,1)S(1)} collective-permute-done((bf16[2,512,128]{2,1,0:T(8,128)(2,1)S(1)}, bf16[2,512,128]{2,1,0:T(8,128)(2,1)S(1)}, u32[]{:S(2)}, u32[]{:S(2)}) %collective-permute-start) | collective-permute-done | bytes 262176 | tf_op jit(solution)/shard_map/ppermute | solution.py:406
  17.2 0.0 collective-permute-done.1.halo_other
  17.2 4.3 %shard_map.97 = (bf16[2,1024,256]{2,1,0:T(8,128)(2,1)S(1)}, bf16[2,512,128]{2,1,0:T(8,128)(2,1)}, bf16[2,512,128]{2,1,0:T(8,128)(2,1)}, f32[8,48,384]{2,1,0:T(8,128)S(1)}, bf16[7,512,128]{2,1,0:T(8,128)(2,1)S(1)}) custom-call(s32[1]{0:T(128)} %bitcast.core, s32[1]{0:T(128)} %bitcast.1.chip, bf16[2,512,128]{2,1,0:T(8,128)(2,1)S(1)} %collective-permute-done.halo_same, ...), custom_call_target="tpu_custom_call" | custom-call | flops 1 | bytes 1 | tf_op jit(solution)/shard_map/pallas_call | solution.py:459
  21.5 0.4 collective-permute-start.3
  21.9 0.2 collective-permute-start.4
  22.1 1.5 %collective-permute-start.5 = (bf16[2,512,128]{2,1,0:T(8,128)(2,1)}, bf16[2,512,128]{2,1,0:T(8,128)(2,1)S(1)}, u32[]{:S(2)}, u32[]{:S(2)}) collective-permute-start(bf16[2,512,128]{2,1,0:T(8,128)(2,1)} %get-tuple-element.34), channel_id=1, source_target_pairs={{1,2},{2,1},{3,4},{4,3},{5,6},{6,5},{7,8},{8,7},{9,10},{10,9},{11,... | collective-permute-start | bytes 786440 | tf_op jit(solution)/shard_map/ppermute | solution.py:483
  23.6 0.4 %collective-permute-done.3.across = bf16[7,512,128]{2,1,0:T(8,128)(2,1)S(1)} collective-permute-done((bf16[7,512,128]{2,1,0:T(8,128)(2,1)S(1)}, bf16[7,512,128]{2,1,0:T(8,128)(2,1)S(1)}, u32[]{:S(2)}, u32[]{:S(2)}) %collective-permute-start.3) | collective-permute-done | bytes 917536 | tf_op jit(solution)/shard_map/ppermute | solution.py:485
  24.1 0.8 %shard_map.99 = bf16[8,48,384]{2,1,0:T(8,128)(2,1)} custom-call(f32[8,48,384]{2,1,0:T(8,128)S(1)} %get-tuple-element.37.keep, bf16[7,512,128]{2,1,0:T(8,128)(2,1)S(1)} %collective-permute-done.3.across), custom_call_target="tpu_custom_call" | custom-call | flops 1 | bytes 1 | tf_op jit(solution)/shard_map/pallas_call | solution.py:487
  24.9 5.9 %all-to-all-start = ((bf16[8,48,384]{2,1,0:T(8,128)(2,1)}), bf16[8,48,384]{2,1,0:T(8,128)(2,1)S(1)}, u32[]{:S(2)}, u32[]{:S(2)}) async-start(bf16[8,48,384]{2,1,0:T(8,128)(2,1)} %shard_map.99), calls=%async_computation | async-start | bytes 589824 | tf_op jit(solution)/shard_map/all_to_all | solution.py:501
  30.7 0.0 collective-permute-done.4.edge_same
  30.7 0.0 collective-permute-done.5.edge_other
  30.7 1.7 %shard_map.98 = (bf16[2,512,128]{2,1,0:T(8,128)(2,1)}, bf16[2,512,128]{2,1,0:T(8,128)(2,1)}, f32[8,128]{1,0:T(8,128)S(1)}) custom-call(s32[1]{0:T(128)} %bitcast.core, s32[1]{0:T(128)} %bitcast.1.chip, bf16[2,1024,256]{2,1,0:T(8,128)(2,1)S(1)} %get-tuple-element.31.whole_grad, bf16[768,384]{1,0:T(8,128)(2,1)S(1)} %get-tuple-element.30.taps, ...), custom_call_target="tpu_custom_call" | custom-call | flops 99999997952 | bytes 1 | tf_op jit(solution)/shard_map/pallas_call | solution.py:502
  32.4 8.7 %all-to-all-done.parts = bf16[8,48,384]{2,1,0:T(8,128)(2,1)S(1)} async-done(((bf16[8,48,384]{2,1,0:T(8,128)(2,1)}), bf16[8,48,384]{2,1,0:T(8,128)(2,1)S(1)}, u32[]{:S(2)}, u32[]{:S(2)}) %all-to-all-start) | async-done | bytes 294944 | tf_op jit(solution)/shard_map/all_to_all | solution.py:501
  41.1 0.1 collective-permute-start.6
  41.2 1.3 %collective-permute-done.6.got = f32[48,384]{1,0:T(8,128)S(1)} collective-permute-done((f32[48,384]{1,0:T(8,128)S(1)}, f32[48,384]{1,0:T(8,128)S(1)}, u32[]{:S(2)}, u32[]{:S(2)}) %collective-permute-start.6) | collective-permute-done | bytes 73760 | tf_op jit(solution)/shard_map/ppermute | solution.py:523
  42.5 0.7 %shard_map.101 = f32[32,1152]{1,0:T(8,128)} custom-call(s32[1]{0:T(128)} %bitcast.core, f32[48,384]{1,0:T(8,128)S(1)} %shard_map.100.mine, f32[48,384]{1,0:T(8,128)S(1)} %collective-permute-done.6.got), custom_call_target="tpu_custom_call" | custom-call | flops 1 | bytes 1 | tf_op jit(solution)/shard_map/pallas_call | solution.py:525
  (1 shorter events, 0.0 us)
Async XLA Ops:
  2.2 15.0 %collective-permute-start = (bf16[2,512,128]{2,1,0:T(8,128)(2,1)S(1)}, bf16[2,512,128]{2,1,0:T(8,128)(2,1)S(1)}, u32[]{:S(2)}, u32[]{:S(2)}) collective-permute-start(bf16[2,512,128]{2,1,0:T(8,128)(2,1)S(1)} %get-tuple-element.21), channel_id=1, source_target_pairs={{0,2},{3,1},{2,4},{5,3},{4,6},{7,5},{6,8},{9,7},{8,10},{11,9},{10,... | collective-permute-start | bytes 786440 | tf_op jit(solution)/shard_map/ppermute | solution.py:406
  5.2 12.0 %collective-permute-start.1 = (bf16[2,512,128]{2,1,0:T(8,128)(2,1)S(1)}, bf16[2,512,128]{2,1,0:T(8,128)(2,1)S(1)}, u32[]{:S(2)}, u32[]{:S(2)}) collective-permute-start(bf16[2,512,128]{2,1,0:T(8,128)(2,1)S(1)} %get-tuple-element.22), channel_id=1, source_target_pairs={{1,2},{2,1},{3,4},{4,3},{5,6},{6,5},{7,8},{8,7},{9,10},{10,9},{11,... | collective-permute-start | bytes 786440 | tf_op jit(solution)/shard_map/ppermute | solution.py:405
  6.7 2.7 %collective-permute-start.2 = (bf16[3968,128]{1,0:T(8,128)(2,1)S(1)}, bf16[3968,128]{1,0:T(8,128)(2,1)}, u32[]{:S(2)}, u32[]{:S(2)}) collective-permute-start(bf16[3968,128]{1,0:T(8,128)(2,1)S(1)} %get-tuple-element.23), channel_id=1, source_target_pairs={{0,1},{1,0},{2,3},{3,2},{4,5},{5,4},{6,7},{7,6},{8,9},{9,8},{10,11... | collective-permute-start | bytes 3047432 | tf_op jit(solution)/shard_map/ppermute | solution.py:407
  21.5 2.5 %collective-permute-start.3 = (bf16[7,512,128]{2,1,0:T(8,128)(2,1)S(1)}, bf16[7,512,128]{2,1,0:T(8,128)(2,1)S(1)}, u32[]{:S(2)}, u32[]{:S(2)}) collective-permute-start(bf16[7,512,128]{2,1,0:T(8,128)(2,1)S(1)} %get-tuple-element.32), channel_id=1, source_target_pairs={{0,1},{1,0},{2,3},{3,2},{4,5},{5,4},{6,7},{7,6},{8,9},{9,8},{10,11... | collective-permute-start | bytes 2752520 | tf_op jit(solution)/shard_map/ppermute | solution.py:485
  21.9 8.8 %collective-permute-start.4 = (bf16[2,512,128]{2,1,0:T(8,128)(2,1)}, bf16[2,512,128]{2,1,0:T(8,128)(2,1)S(1)}, u32[]{:S(2)}, u32[]{:S(2)}) collective-permute-start(bf16[2,512,128]{2,1,0:T(8,128)(2,1)} %get-tuple-element.33), channel_id=1, source_target_pairs={{2,0},{1,3},{4,2},{3,5},{6,4},{5,7},{8,6},{7,9},{10,8},{9,11},{12,... | collective-permute-start | bytes 786440 | tf_op jit(solution)/shard_map/ppermute | solution.py:484
  22.1 8.6 %collective-permute-start.5 = (bf16[2,512,128]{2,1,0:T(8,128)(2,1)}, bf16[2,512,128]{2,1,0:T(8,128)(2,1)S(1)}, u32[]{:S(2)}, u32[]{:S(2)}) collective-permute-start(bf16[2,512,128]{2,1,0:T(8,128)(2,1)} %get-tuple-element.34), channel_id=1, source_target_pairs={{1,2},{2,1},{3,4},{4,3},{5,6},{6,5},{7,8},{8,7},{9,10},{10,9},{11,... | collective-permute-start | bytes 786440 | tf_op jit(solution)/shard_map/ppermute | solution.py:483
  24.9 16.2 %all-to-all-start = ((bf16[8,48,384]{2,1,0:T(8,128)(2,1)}), bf16[8,48,384]{2,1,0:T(8,128)(2,1)S(1)}, u32[]{:S(2)}, u32[]{:S(2)}) async-start(bf16[8,48,384]{2,1,0:T(8,128)(2,1)} %shard_map.99), calls=%async_computation | async-start | bytes 589824 | tf_op jit(solution)/shard_map/all_to_all | solution.py:501
  41.1 1.3 %collective-permute-start.6 = (f32[48,384]{1,0:T(8,128)S(1)}, f32[48,384]{1,0:T(8,128)S(1)}, u32[]{:S(2)}, u32[]{:S(2)}) collective-permute-start(f32[48,384]{1,0:T(8,128)S(1)} %shard_map.100.mine), channel_id=1, source_target_pairs={{0,1},{1,0},{2,3},{3,2},{4,5},{5,4},{6,7},{7,6},{8,9},{9,8},{10,11... | collective-permute-start | bytes 221192 | tf_op jit(solution)/shard_map/ppermute | solution.py:523

commit v4 on v3

--- a/solution.py
+++ b/solution.py
@@ -68,15 +68,19 @@
     return moves
 
 
-def first_kernel(
-    core, left, right, zero, one, two, three,
-    own, near, pack, sems,
-):
-    c = core[0]
-    half = left.shape[1]
+def first_kernel(core, left, right, own, near, sems):
+    c = core[0]
     moves = []
     for image, source in enumerate((left, right)):
         moves += [(source.at[c], own.at[image]), (source.at[1 - c], near.at[image])]
+    for copy in started(moves, sems):
+        copy.wait()
+
+
+def pack_kernel(core, left, right, zero, one, two, three, _, pack, sems):
+    c = core[0]
+    half = left.shape[1]
+    moves = []
     for index, source in enumerate((left.at[c], left.at[1 - c], right.at[c], right.at[1 - c])):
         moves.append((source, pack.at[pl.ds(index * half, half)]))
     moves += level_moves([x.at[1 - c] for x in (zero, one, two, three)], pack, 4 * half)
@@ -199,7 +203,7 @@
 
 
 def main_kernel(
-    chips, core, chip, halo_same, halo_other, weight, own_sum, images_t, band, band_t, taps,
+    chips, core, chip, halo_other, halo_same, weight, own_sum, images_t, band, band_t, taps,
     whole_grad, edge_same, edge_other, wg_keep, across,
     padded, feats, wide, grads, wg, edges, edge_sems,
 ):
@@ -318,31 +322,34 @@
                 ]
 
 
-def finish_kernel(
-    chips, core, chip, whole_grad, taps, across, edge_same, edge_other,
-    left, right, token,
-    wide, part,
-):
-    c = core[0]
-    half, channels = left.shape[1], left.shape[2]
+def keep_kernel(core, whole_grad, taps, _, out, wide, part):
+    c = core[0]
+    half, channels = out.shape[1], out.shape[2]
     size = whole_grad.shape[1]
     here = pl.multiple_of(c * half, half)
-    other_alone = at_end(chips, chip[0], c == 1)
-    same_alone = at_end(chips, chip[0], c == 0)
     clear_pads(wide, size)
-    for image, out in enumerate((left, right)):
+    for image in range(2):
         wide[pl.ds(PAD, size)] = whole_grad[image].astype(F32)
         part[...] = wide[pl.ds(here, half + 2 * PAD)]
         grads = jnp.concatenate(
             [part[pl.ds(PAD + by, half)].astype(BF) for by in (1, 0, -1)], axis=1
         )
         pair = dot(grads, taps[:, pl.ds(channels, 2 * channels)])
-        for role, row, edge, alone in (
-            (0, c, edge_other, other_alone),
-            (1, 1 - c, edge_same, same_alone),
-        ):
+        for role, row in ((0, c), (1, 1 - c)):
+            out[2 * image + row] = pair[:, role * channels : (role + 1) * channels]
+
+
+def finish_kernel(
+    chips, core, chip, keep, across, edge_other, edge_same,
+    left, right, token,
+):
+    c = core[0]
+    other_alone = at_end(chips, chip[0], c == 1)
+    same_alone = at_end(chips, chip[0], c == 0)
+    for image, out in enumerate((left, right)):
+        for row, edge, alone in ((c, edge_other, other_alone), (1 - c, edge_same, same_alone)):
             out[row] = (
-                pair[:, role * channels : (role + 1) * channels]
+                keep[2 * image + row]
                 + across[2 * image + row].astype(F32)
                 + jnp.where(alone, 0.0, edge[image].astype(F32))
             ).astype(BF)
@@ -393,15 +400,24 @@
     any_space = pl.BlockSpec(memory_space=pl.ANY)
     level_rows = band * (reach + reach // 2 + reach // 4 + reach // 8) // channels
     level_copies = (reach + reach // 2) // channels + 2 * (band // channels)
-    own, near, pack = pl.pallas_call(
+    own, near = pl.pallas_call(
         first_kernel,
-        out_shape=(row_shape,) * 2 + (shape((4 * band + level_rows, channels), BF),),
-        in_specs=[SCALAR] + [any_space] * 6,
-        out_specs=vmem(3),
-        scratch_shapes=[pltpu.SemaphoreType.DMA((8 + level_copies,))],
+        out_shape=(row_shape,) * 2,
+        in_specs=[SCALAR] + [any_space] * 2,
+        out_specs=vmem(2),
+        scratch_shapes=[pltpu.SemaphoreType.DMA((4,))],
         cost_estimate=SMALL,
         compiler_params=params(2),
-    )(core, *in_hbm[:6])
+    )(core, *in_hbm[:2])
+    pack = pl.pallas_call(
+        pack_kernel,
+        out_shape=shape((4 * band + level_rows, channels), BF),
+        in_specs=[SCALAR] + [any_space] * 7,
+        out_specs=vmem(1)[0],
+        scratch_shapes=[pltpu.SemaphoreType.DMA((4 + level_copies,))],
+        cost_estimate=SMALL,
+        compiler_params=params(2),
+    )(core, *in_hbm[:6], own)
     halo_other = lax.ppermute(own, flat, other)
     halo_same = lax.ppermute(near, flat, same_in)
     got = pltpu.with_memory_space_constraint(lax.ppermute(pack, "cols", swap), pltpu.HBM)
@@ -478,7 +494,7 @@
         ],
         cost_estimate=SMALL,
         compiler_params=params(16),
-    )(core, chip_at, halo_same, halo_other, outer_weight, own_sum, images_t, skew, skew_t, taps)
+    )(core, chip_at, halo_other, halo_same, outer_weight, own_sum, images_t, skew, skew_t, taps)
 
     got_other = lax.ppermute(edge_other, flat, other)
     got_same = lax.ppermute(edge_same, flat, same_out)
@@ -499,18 +515,26 @@
         theirs = lax.dynamic_index_in_dim(halves, cores - 1 - core[0], 0, False).astype(BF)
         chip_wg = (mine + lax.ppermute(theirs, "cols", swap).astype(F32)).astype(BF)
     parts = lax.all_to_all(chip_wg, "rows", 0, 0, tiled=False)
-    grad_left, grad_right, token = pl.pallas_call(
-        functools.partial(finish_kernel, chips),
-        out_shape=(shape(left_image.shape, BF),) * 2 + (shape((8, 128), F32),),
-        in_specs=[SCALAR] * 2 + vmem(5),
-        out_specs=vmem(3),
+    kept = pl.pallas_call(
+        keep_kernel,
+        out_shape=shape((4, band, channels), F32),
+        in_specs=[SCALAR] + vmem(2) + [any_space],
+        out_specs=vmem(1)[0],
         scratch_shapes=[
             pltpu.VMEM((size + 2 * PAD, features), F32),
             pltpu.VMEM((band + 2 * PAD, features), F32),
         ],
+        cost_estimate=SMALL,
+        compiler_params=params(8),
+    )(core, whole_grad, taps, across_got)
+    grad_left, grad_right, token = pl.pallas_call(
+        functools.partial(finish_kernel, chips),
+        out_shape=(shape(left_image.shape, BF),) * 2 + (shape((8, 128), F32),),
+        in_specs=[SCALAR] * 2 + vmem(4),
+        out_specs=vmem(3),
         cost_estimate=LARGE,
-        compiler_params=params(8),
-    )(core, chip_at, whole_grad, taps, across_got, got_same, got_other)
+        compiler_params=params(4),
+    )(core, chip_at, kept, across_got, got_other, got_same)
     scale = 1.0 / math.sqrt(2 * depth * band * chips * cores)
     mine = pl.pallas_call(
         functools.partial(sum_kernel, scale),

time: 43.5 us -> 42.5 us (0.977)
  waiting for transfers between devices: 15.2 us -> 12.1 us
  starting transfers between devices: 12.7 us -> 13.8 us
  Pallas kernels: 14.5 us -> 15.6 us
    pallas_call x1 -> x3, Pallas kernels: 1.59 us -> 3.33 us  [the longest x1 1.38 us: on_device(): pl.pallas_call(pack_kernel, out_shape=shape((4 * band + level_rows, chann...]
    ppermute x1, waiting for transfers between devices: 4.17 us -> 2.72 us  [on_device(): halo_same = lax.ppermute(near, flat, same_in)]
    all_to_all x1, waiting for transfers between devices: 8.69 us -> 7.51 us  [on_device(): parts = lax.all_to_all(chip_wg, 'rows', 0, 0, tiled=False)]
    ppermute x1, starting transfers between devices: 0.21 us -> 0.94 us  [on_device(): got_same = lax.ppermute(edge_same, flat, same_out)]
    pallas_call x1, Pallas kernels: 1.67 us -> 0.95 us  [on_device(): pl.pallas_call(functools.partial(finish_kernel, chips), out_shape=(shape(...]
    ppermute x1, waiting for transfers between devices: 0.45 us -> 0.01 us  [on_device(): across_got = lax.ppermute(across, 'cols', swap)]
  transfers between devices with their start and end apart: 8 -> 8, of which waited for: 5 -> 4; matrix products, arithmetic and copies ran while one was open for 0% -> 0% of each run, Pallas kernels for 18% -> 22%
where the time goes in v4:
time: 42.5 us; the launch traced here: 42.2 us
  Pallas kernels  15.6 us (37%)
  starting transfers between devices  13.8 us (32%)
  waiting for transfers between devices  12.1 us (28%)
  between operations  0.72 us (2%)
    all_to_all x1, waiting for transfers between devices, on_device(): parts = lax.all_to_all(chip_wg, 'rows', 0, 0, tiled=False)  7.51 us
    all_to_all x1, starting transfers between devices, on_device(): parts = lax.all_to_all(chip_wg, 'rows', 0, 0, tiled=False)  6.14 us
    pallas_call x1, Pallas kernels, on_device(): pl.pallas_call(functools.partial(main_kernel, chips), out_shape=(shape((2...  4.3 us
    pallas_call x1, Pallas kernels, on_device(): pl.pallas_call(prepare_kernel, out_shape=(shape((2, size, features), F32)...  3.54 us
    ppermute x1, starting transfers between devices, on_device(): halo_same = lax.ppermute(near, flat, same_in)  3 us
    ppermute x1, waiting for transfers between devices, on_device(): halo_same = lax.ppermute(near, flat, same_in)  2.72 us
    pallas_call x1, Pallas kernels, on_device(): pl.pallas_call(local_kernel, out_shape=(shape((band, reach), BF), shape((...  1.94 us
    ppermute x1, starting transfers between devices, on_device(): got_other = lax.ppermute(edge_other, flat, other)  1.53 us
  transfers between devices with their start and end apart: 8, of which 4 were waited for; matrix products, arithmetic and copies ran while one was open for 0% of the time, Pallas kernels for 22%

profile of v4, /device:TPU:0, one launch (start us, length us, event | category | flops | bytes accessed | tf_op | source)
XLA Modules:
  0.0 42.2 jit_solution(991588806966202690)
XLA Ops:
  0.6 1.1 %shard_map.94 = (bf16[2,512,128]{2,1,0:T(8,128)(2,1)S(1)}, bf16[2,512,128]{2,1,0:T(8,128)(2,1)S(1)}) custom-call(s32[1]{0:T(128)} %bitcast.core, bf16[2,512,128]{2,1,0:T(8,128)(2,1)} %left.5, bf16[2,512,128]{2,1,0:T(8,128)(2,1)} %right.5), custom_call_target="tpu_custom_call" | custom-call | flops 1 | bytes 1 | tf_op jit(solution)/shard_map/pallas_call | solution.py:403
  1.8 3.0 %collective-permute-start.1 = (bf16[2,512,128]{2,1,0:T(8,128)(2,1)S(1)}, bf16[2,512,128]{2,1,0:T(8,128)(2,1)S(1)}, u32[]{:S(2)}, u32[]{:S(2)}) collective-permute-start(bf16[2,512,128]{2,1,0:T(8,128)(2,1)S(1)} %get-tuple-element.21), channel_id=1, source_target_pairs={{0,2},{3,1},{2,4},{5,3},{4,6},{7,5},{6,8},{9,7},{8,10},{11,9},{10,... | collective-permute-start | bytes 786440 | tf_op jit(solution)/shard_map/ppermute | solution.py:422
  4.8 1.5 %collective-permute-start = (bf16[2,512,128]{2,1,0:T(8,128)(2,1)S(1)}, bf16[2,512,128]{2,1,0:T(8,128)(2,1)S(1)}, u32[]{:S(2)}, u32[]{:S(2)}) collective-permute-start(bf16[2,512,128]{2,1,0:T(8,128)(2,1)S(1)} %get-tuple-element.20._), channel_id=1, source_target_pairs={{1,2},{2,1},{3,4},{4,3},{5,6},{6,5},{7,8},{8,7},{9,10},{10,9},{11,... | collective-permute-start | bytes 786440 | tf_op jit(solution)/shard_map/ppermute | solution.py:421
  6.3 1.4 %shard_map.95 = bf16[3968,128]{1,0:T(8,128)(2,1)S(1)} custom-call(s32[1]{0:T(128)} %bitcast.core, bf16[2,512,128]{2,1,0:T(8,128)(2,1)} %left.5, bf16[2,512,128]{2,1,0:T(8,128)(2,1)} %right.5, bf16[2,512,256]{2,1,0:T(8,128)(2,1)} %zero_hbm.1, bf16[2,512,128]{2,1,0:T(8,128)(2,1)} %one_hbm.1, bf16[2,64,512]{2,1,0:T(8,128)(2,1)} %bitcast.7, ...), custom_call_target="tpu_custom_call" | custom-call | flops 1 | bytes 1 | tf_op jit(solution)/shard_map/pallas_call | solution.py:412
  7.7 0.2 collective-permute-start.2
  7.9 1.9 %shard_map.96 = (bf16[512,256]{1,0:T(8,128)(2,1)S(1)}, bf16[768,384]{1,0:T(8,128)(2,1)S(1)}) custom-call(s32[1]{0:T(128)} %bitcast.core, bf16[3,384,256]{2,1,0:T(8,128)(2,1)} %bitcast.5, bf16[2,512,256]{2,1,0:T(8,128)(2,1)} %zero_hbm.1, bf16[2,512,128]{2,1,0:T(8,128)(2,1)} %one_hbm.1, bf16[2,64,512]{2,1,0:T(8,128)(2,1)} %bitcast.8, bf16[2,32,512]{2,1,0:T(8,128)(2,1)} %bitcast.10), custom_call_target="tpu_custom_call" | custom-call | flops 99999997952 | bytes 1 | tf_op jit(solution)/shard_map/pallas_call | solution.py:425
  9.8 0.7 %collective-permute-done.2.got = bf16[3968,128]{1,0:T(8,128)(2,1)} collective-permute-done((bf16[3968,128]{1,0:T(8,128)(2,1)S(1)}, bf16[3968,128]{1,0:T(8,128)(2,1)}, u32[]{:S(2)}, u32[]{:S(2)}) %collective-permute-start.2) | collective-permute-done | bytes 1015840 | tf_op jit(solution)/shard_map/ppermute | solution.py:423
  10.5 3.5 %shard_map.97 = (f32[2,1024,256]{2,1,0:T(8,128)S(1)}, bf16[2,256,1024]{2,1,0:T(8,128)(2,1)S(1)}, bf16[4,256,512]{2,1,0:T(8,128)(2,1)S(1)}, bf16[4,512,256]{2,1,0:T(8,128)(2,1)S(1)}, bf16[384,256]{1,0:T(8,128)(2,1)S(1)}) custom-call(s32[1]{0:T(128)} %bitcast.core, bf16[2,512,128]{2,1,0:T(8,128)(2,1)} %left.5, bf16[2,512,128]{2,1,0:T(8,128)(2,1)} %right.5, ...), custom_call_target="tpu_custom_call" | custom-call | flops 1 | bytes 1 | tf_op jit(solution)/shard_map/pallas_call | solution.py:444
  14.0 2.7 %collective-permute-done.1.halo_same = bf16[2,512,128]{2,1,0:T(8,128)(2,1)S(1)} collective-permute-done((bf16[2,512,128]{2,1,0:T(8,128)(2,1)S(1)}, bf16[2,512,128]{2,1,0:T(8,128)(2,1)S(1)}, u32[]{:S(2)}, u32[]{:S(2)}) %collective-permute-start.1) | collective-permute-done | bytes 262176 | tf_op jit(solution)/shard_map/ppermute | solution.py:422
  16.8 0.0 collective-permute-done.halo_other
  16.8 4.3 %shard_map.98 = (bf16[2,1024,256]{2,1,0:T(8,128)(2,1)S(1)}, bf16[2,512,128]{2,1,0:T(8,128)(2,1)}, bf16[2,512,128]{2,1,0:T(8,128)(2,1)}, f32[8,48,384]{2,1,0:T(8,128)S(1)}, bf16[7,512,128]{2,1,0:T(8,128)(2,1)S(1)}) custom-call(s32[1]{0:T(128)} %bitcast.core, s32[1]{0:T(128)} %bitcast.1.chip, bf16[2,512,128]{2,1,0:T(8,128)(2,1)S(1)} %collective-permute-done.halo_other, ...), custom_call_target="tpu_custom_call" | custom-call | flops 1 | bytes 1 | tf_op jit(solution)/shard_map/pallas_call | solution.py:475
  21.1 0.4 collective-permute-start.3
  21.4 1.5 %collective-permute-start.4 = (bf16[2,512,128]{2,1,0:T(8,128)(2,1)}, bf16[2,512,128]{2,1,0:T(8,128)(2,1)S(1)}, u32[]{:S(2)}, u32[]{:S(2)}) collective-permute-start(bf16[2,512,128]{2,1,0:T(8,128)(2,1)} %get-tuple-element.31), channel_id=1, source_target_pairs={{1,2},{2,1},{3,4},{4,3},{5,6},{6,5},{7,8},{8,7},{9,10},{10,9},{11,... | collective-permute-start | bytes 786440 | tf_op jit(solution)/shard_map/ppermute | solution.py:499
  23.0 0.9 %collective-permute-start.5 = (bf16[2,512,128]{2,1,0:T(8,128)(2,1)}, bf16[2,512,128]{2,1,0:T(8,128)(2,1)S(1)}, u32[]{:S(2)}, u32[]{:S(2)}) collective-permute-start(bf16[2,512,128]{2,1,0:T(8,128)(2,1)} %get-tuple-element.32), channel_id=1, source_target_pairs={{2,0},{1,3},{4,2},{3,5},{6,4},{5,7},{8,6},{7,9},{10,8},{9,11},{12,... | collective-permute-start | bytes 786440 | tf_op jit(solution)/shard_map/ppermute | solution.py:500
  23.9 0.0 collective-permute-done.3._.across
  23.9 0.8 %shard_map.101 = bf16[8,48,384]{2,1,0:T(8,128)(2,1)} custom-call(f32[8,48,384]{2,1,0:T(8,128)S(1)} %get-tuple-element.35.keep, bf16[7,512,128]{2,1,0:T(8,128)(2,1)S(1)} %collective-permute-done.3._.across), custom_call_target="tpu_custom_call" | custom-call | flops 1 | bytes 1 | tf_op jit(solution)/shard_map/pallas_call | solution.py:503
  24.7 6.1 %all-to-all-start = ((bf16[8,48,384]{2,1,0:T(8,128)(2,1)}), bf16[8,48,384]{2,1,0:T(8,128)(2,1)S(1)}, u32[]{:S(2)}, u32[]{:S(2)}) async-start(bf16[8,48,384]{2,1,0:T(8,128)(2,1)} %shard_map.101), calls=%async_computation | async-start | bytes 589824 | tf_op jit(solution)/shard_map/all_to_all | solution.py:517
  30.8 0.8 %shard_map.99.keep = f32[4,512,128]{2,1,0:T(8,128)S(1)} custom-call(s32[1]{0:T(128)} %bitcast.core, bf16[2,1024,256]{2,1,0:T(8,128)(2,1)S(1)} %get-tuple-element.29.whole_grad, bf16[768,384]{1,0:T(8,128)(2,1)S(1)} %get-tuple-element.28.taps, bf16[7,512,128]{2,1,0:T(8,128)(2,1)S(1)} %collective-permute-done.3._.across), custom_call_target="tpu_custom_call" | custom-call | flops 1 | bytes 1 | tf_op jit(solution)/shard_map/pallas_call | solution.py:518
  31.7 0.0 collective-permute-done.4.edge_other
  31.7 0.0 collective-permute-done.5.edge_same
  31.7 1.0 %shard_map.100 = (bf16[2,512,128]{2,1,0:T(8,128)(2,1)}, bf16[2,512,128]{2,1,0:T(8,128)(2,1)}, f32[8,128]{1,0:T(8,128)S(1)}) custom-call(s32[1]{0:T(128)} %bitcast.core, s32[1]{0:T(128)} %bitcast.1.chip, f32[4,512,128]{2,1,0:T(8,128)S(1)} %shard_map.99.keep, bf16[7,512,128]{2,1,0:T(8,128)(2,1)S(1)} %collective-permute-done.3._.across, ...), custom_call_target="tpu_custom_call" | custom-call | flops 99999997952 | bytes 1 | tf_op jit(solution)/shard_map/pallas_call | solution.py:530
  32.6 7.5 %all-to-all-done.parts = bf16[8,48,384]{2,1,0:T(8,128)(2,1)S(1)} async-done(((bf16[8,48,384]{2,1,0:T(8,128)(2,1)}), bf16[8,48,384]{2,1,0:T(8,128)(2,1)S(1)}, u32[]{:S(2)}, u32[]{:S(2)}) %all-to-all-start) | async-done | bytes 294944 | tf_op jit(solution)/shard_map/all_to_all | solution.py:517
  40.2 0.1 collective-permute-start.6
  40.3 1.3 %collective-permute-done.6.got = f32[48,384]{1,0:T(8,128)S(1)} collective-permute-done((f32[48,384]{1,0:T(8,128)S(1)}, f32[48,384]{1,0:T(8,128)S(1)}, u32[]{:S(2)}, u32[]{:S(2)}) %collective-permute-start.6) | collective-permute-done | bytes 73760 | tf_op jit(solution)/shard_map/ppermute | solution.py:547
  41.5 0.7 %shard_map.103 = f32[32,1152]{1,0:T(8,128)} custom-call(s32[1]{0:T(128)} %bitcast.core, f32[48,384]{1,0:T(8,128)S(1)} %shard_map.102.mine, f32[48,384]{1,0:T(8,128)S(1)} %collective-permute-done.6.got), custom_call_target="tpu_custom_call" | custom-call | flops 1 | bytes 1 | tf_op jit(solution)/shard_map/pallas_call | solution.py:549
  (1 shorter events, 0.0 us)
Async XLA Ops:
  1.8 15.0 %collective-permute-start.1 = (bf16[2,512,128]{2,1,0:T(8,128)(2,1)S(1)}, bf16[2,512,128]{2,1,0:T(8,128)(2,1)S(1)}, u32[]{:S(2)}, u32[]{:S(2)}) collective-permute-start(bf16[2,512,128]{2,1,0:T(8,128)(2,1)S(1)} %get-tuple-element.21), channel_id=1, source_target_pairs={{0,2},{3,1},{2,4},{5,3},{4,6},{7,5},{6,8},{9,7},{8,10},{11,9},{10,... | collective-permute-start | bytes 786440 | tf_op jit(solution)/shard_map/ppermute | solution.py:422
  4.8 12.0 %collective-permute-start = (bf16[2,512,128]{2,1,0:T(8,128)(2,1)S(1)}, bf16[2,512,128]{2,1,0:T(8,128)(2,1)S(1)}, u32[]{:S(2)}, u32[]{:S(2)}) collective-permute-start(bf16[2,512,128]{2,1,0:T(8,128)(2,1)S(1)} %get-tuple-element.20._), channel_id=1, source_target_pairs={{1,2},{2,1},{3,4},{4,3},{5,6},{6,5},{7,8},{8,7},{9,10},{10,9},{11,... | collective-permute-start | bytes 786440 | tf_op jit(solution)/shard_map/ppermute | solution.py:421
  7.7 2.8 %collective-permute-start.2 = (bf16[3968,128]{1,0:T(8,128)(2,1)S(1)}, bf16[3968,128]{1,0:T(8,128)(2,1)}, u32[]{:S(2)}, u32[]{:S(2)}) collective-permute-start(bf16[3968,128]{1,0:T(8,128)(2,1)S(1)} %shard_map.95), channel_id=1, source_target_pairs={{0,1},{1,0},{2,3},{3,2},{4,5},{5,4},{6,7},{7,6},{8,9},{9,8},{10,11... | collective-permute-start | bytes 3047432 | tf_op jit(solution)/shard_map/ppermute | solution.py:423
  21.1 2.8 %collective-permute-start.3 = (bf16[7,512,128]{2,1,0:T(8,128)(2,1)S(1)}, bf16[7,512,128]{2,1,0:T(8,128)(2,1)S(1)}, u32[]{:S(2)}, u32[]{:S(2)}) collective-permute-start(bf16[7,512,128]{2,1,0:T(8,128)(2,1)S(1)} %get-tuple-element.30), channel_id=1, source_target_pairs={{0,1},{1,0},{2,3},{3,2},{4,5},{5,4},{6,7},{7,6},{8,9},{9,8},{10,11... | collective-permute-start | bytes 2752520 | tf_op jit(solution)/shard_map/ppermute | solution.py:501
  21.4 10.2 %collective-permute-start.4 = (bf16[2,512,128]{2,1,0:T(8,128)(2,1)}, bf16[2,512,128]{2,1,0:T(8,128)(2,1)S(1)}, u32[]{:S(2)}, u32[]{:S(2)}) collective-permute-start(bf16[2,512,128]{2,1,0:T(8,128)(2,1)} %get-tuple-element.31), channel_id=1, source_target_pairs={{1,2},{2,1},{3,4},{4,3},{5,6},{6,5},{7,8},{8,7},{9,10},{10,9},{11,... | collective-permute-start | bytes 786440 | tf_op jit(solution)/shard_map/ppermute | solution.py:499
  23.0 8.7 %collective-permute-start.5 = (bf16[2,512,128]{2,1,0:T(8,128)(2,1)}, bf16[2,512,128]{2,1,0:T(8,128)(2,1)S(1)}, u32[]{:S(2)}, u32[]{:S(2)}) collective-permute-start(bf16[2,512,128]{2,1,0:T(8,128)(2,1)} %get-tuple-element.32), channel_id=1, source_target_pairs={{2,0},{1,3},{4,2},{3,5},{6,4},{5,7},{8,6},{7,9},{10,8},{9,11},{12,... | collective-permute-start | bytes 786440 | tf_op jit(solution)/shard_map/ppermute | solution.py:500
  24.7 15.5 %all-to-all-start = ((bf16[8,48,384]{2,1,0:T(8,128)(2,1)}), bf16[8,48,384]{2,1,0:T(8,128)(2,1)S(1)}, u32[]{:S(2)}, u32[]{:S(2)}) async-start(bf16[8,48,384]{2,1,0:T(8,128)(2,1)} %shard_map.101), calls=%async_computation | async-start | bytes 589824 | tf_op jit(solution)/shard_map/all_to_all | solution.py:517
  40.2 1.3 %collective-permute-start.6 = (f32[48,384]{1,0:T(8,128)S(1)}, f32[48,384]{1,0:T(8,128)S(1)}, u32[]{:S(2)}, u32[]{:S(2)}) collective-permute-start(f32[48,384]{1,0:T(8,128)S(1)} %shard_map.102.mine), channel_id=1, source_target_pairs={{0,1},{1,0},{2,3},{3,2},{4,5},{5,4},{6,7},{7,6},{8,9},{9,8},{10,11... | collective-permute-start | bytes 221192 | tf_op jit(solution)/shard_map/ppermute | solution.py:547

commit v5 on v4

--- a/solution.py
+++ b/solution.py
@@ -292,7 +292,7 @@
                 )
 
 
-def add_kernel(keep, across, out):
+def add_kernel(keep, across, target, out, sems):
     chunks, rows, lanes = keep.shape
     for chunk in range(chunks):
         for tap in range(3):
@@ -300,6 +300,9 @@
             out[chunk, :, part] = (
                 keep[chunk, :, part] + across[4 + tap, pl.ds(chunk * rows, rows)].astype(F32)
             ).astype(BF)
+        pltpu.make_async_copy(out.at[chunk], target.at[chunk], sems.at[chunk]).start()
+    for chunk in range(chunks):
+        pltpu.make_async_copy(out.at[chunk], target.at[chunk], sems.at[chunk]).wait()
 
 
 def sum_kernel(scale, parts, _, out):
@@ -342,17 +345,24 @@
 def finish_kernel(
     chips, core, chip, keep, across, edge_other, edge_same,
     left, right, token,
+    rows, sems,
 ):
     c = core[0]
     other_alone = at_end(chips, chip[0], c == 1)
     same_alone = at_end(chips, chip[0], c == 0)
+    copies = []
     for image, out in enumerate((left, right)):
         for row, edge, alone in ((c, edge_other, other_alone), (1 - c, edge_same, same_alone)):
-            out[row] = (
+            index = len(copies)
+            rows[index] = (
                 keep[2 * image + row]
                 + across[2 * image + row].astype(F32)
                 + jnp.where(alone, 0.0, edge[image].astype(F32))
             ).astype(BF)
+            copies.append(pltpu.make_async_copy(rows.at[index], out.at[row], sems.at[index]))
+            copies[-1].start()
+    for copy in copies:
+        copy.wait()
     token[...] = jnp.zeros_like(token)
 
 
@@ -502,9 +512,10 @@
     if tiled:
         chip_wg = pl.pallas_call(
             add_kernel,
-            out_shape=shape(wg_shape, BF),
+            out_shape=pltpu.HBM(wg_shape, BF),
             in_specs=vmem(2),
-            out_specs=vmem(1)[0],
+            out_specs=any_space,
+            scratch_shapes=[pltpu.VMEM(wg_shape, BF), pltpu.SemaphoreType.DMA((chips,))],
             cost_estimate=SMALL,
             compiler_params=params(4),
         )(wg_keep, across_got)
@@ -529,9 +540,13 @@
     )(core, whole_grad, taps, across_got)
     grad_left, grad_right, token = pl.pallas_call(
         functools.partial(finish_kernel, chips),
-        out_shape=(shape(left_image.shape, BF),) * 2 + (shape((8, 128), F32),),
+        out_shape=(pltpu.HBM(left_image.shape, BF),) * 2 + (shape((8, 128), F32),),
         in_specs=[SCALAR] * 2 + vmem(4),
-        out_specs=vmem(3),
+        out_specs=[any_space] * 2 + vmem(1),
+        scratch_shapes=[
+            pltpu.VMEM((4, band, channels), BF),
+            pltpu.SemaphoreType.DMA((4,)),
+        ],
         cost_estimate=LARGE,
         compiler_params=params(4),
     )(core, chip_at, kept, across_got, got_other, got_same)

time: 42.5 us -> 42.5 us (level)
  no operation moved by 1% of the time
where the time goes in v5:
time: 42.5 us; the launch traced here: 42.1 us
  Pallas kernels  15.4 us (36%)
  starting transfers between devices  13.8 us (32%)
  waiting for transfers between devices  12.2 us (29%)
  between operations  0.74 us (2%)
    all_to_all x1, waiting for transfers between devices, on_device(): parts = lax.all_to_all(chip_wg, 'rows', 0, 0, tiled=False)  7.61 us
    all_to_all x1, starting transfers between devices, on_device(): parts = lax.all_to_all(chip_wg, 'rows', 0, 0, tiled=False)  6.16 us
    pallas_call x1, Pallas kernels, on_device(): pl.pallas_call(functools.partial(main_kernel, chips), out_shape=(shape((2...  4.17 us
    pallas_call x1, Pallas kernels, on_device(): pl.pallas_call(prepare_kernel, out_shape=(shape((2, size, features), F32)...  3.54 us
    ppermute x1, starting transfers between devices, on_device(): halo_same = lax.ppermute(near, flat, same_in)  3 us
    ppermute x1, waiting for transfers between devices, on_device(): halo_same = lax.ppermute(near, flat, same_in)  2.72 us
    pallas_call x1, Pallas kernels, on_device(): pl.pallas_call(local_kernel, out_shape=(shape((band, reach), BF), shape((...  1.94 us
    ppermute x1, starting transfers between devices, on_device(): got_other = lax.ppermute(edge_other, flat, other)  1.52 us
  transfers between devices with their start and end apart: 8, of which 4 were waited for; matrix products, arithmetic and copies ran while one was open for 0% of the time, Pallas kernels for 22%

profile of v5, /device:TPU:0, one launch (start us, length us, event | category | flops | bytes accessed | tf_op | source)
XLA Modules:
  0.0 42.1 jit_solution(11391211258465057474)
XLA Ops:
  0.6 1.1 %shard_map.94 = (bf16[2,512,128]{2,1,0:T(8,128)(2,1)S(1)}, bf16[2,512,128]{2,1,0:T(8,128)(2,1)S(1)}) custom-call(s32[1]{0:T(128)} %bitcast.core, bf16[2,512,128]{2,1,0:T(8,128)(2,1)} %left.5, bf16[2,512,128]{2,1,0:T(8,128)(2,1)} %right.5), custom_call_target="tpu_custom_call" | custom-call | flops 1 | bytes 1 | tf_op jit(solution)/shard_map/pallas_call | solution.py:413
  1.8 3.0 %collective-permute-start.1 = (bf16[2,512,128]{2,1,0:T(8,128)(2,1)S(1)}, bf16[2,512,128]{2,1,0:T(8,128)(2,1)S(1)}, u32[]{:S(2)}, u32[]{:S(2)}) collective-permute-start(bf16[2,512,128]{2,1,0:T(8,128)(2,1)S(1)} %get-tuple-element.21), channel_id=1, source_target_pairs={{0,2},{3,1},{2,4},{5,3},{4,6},{7,5},{6,8},{9,7},{8,10},{11,9},{10,... | collective-permute-start | bytes 786440 | tf_op jit(solution)/shard_map/ppermute | solution.py:432
  4.8 1.5 %collective-permute-start = (bf16[2,512,128]{2,1,0:T(8,128)(2,1)S(1)}, bf16[2,512,128]{2,1,0:T(8,128)(2,1)S(1)}, u32[]{:S(2)}, u32[]{:S(2)}) collective-permute-start(bf16[2,512,128]{2,1,0:T(8,128)(2,1)S(1)} %get-tuple-element.20._), channel_id=1, source_target_pairs={{1,2},{2,1},{3,4},{4,3},{5,6},{6,5},{7,8},{8,7},{9,10},{10,9},{11,... | collective-permute-start | bytes 786440 | tf_op jit(solution)/shard_map/ppermute | solution.py:431
  6.3 1.4 %shard_map.95 = bf16[3968,128]{1,0:T(8,128)(2,1)S(1)} custom-call(s32[1]{0:T(128)} %bitcast.core, bf16[2,512,128]{2,1,0:T(8,128)(2,1)} %left.5, bf16[2,512,128]{2,1,0:T(8,128)(2,1)} %right.5, bf16[2,512,256]{2,1,0:T(8,128)(2,1)} %zero_hbm.1, bf16[2,512,128]{2,1,0:T(8,128)(2,1)} %one_hbm.1, bf16[2,64,512]{2,1,0:T(8,128)(2,1)} %bitcast.7, ...), custom_call_target="tpu_custom_call" | custom-call | flops 1 | bytes 1 | tf_op jit(solution)/shard_map/pallas_call | solution.py:422
  7.7 0.2 collective-permute-start.2
  7.9 1.9 %shard_map.96 = (bf16[512,256]{1,0:T(8,128)(2,1)S(1)}, bf16[768,384]{1,0:T(8,128)(2,1)S(1)}) custom-call(s32[1]{0:T(128)} %bitcast.core, bf16[3,384,256]{2,1,0:T(8,128)(2,1)} %bitcast.5, bf16[2,512,256]{2,1,0:T(8,128)(2,1)} %zero_hbm.1, bf16[2,512,128]{2,1,0:T(8,128)(2,1)} %one_hbm.1, bf16[2,64,512]{2,1,0:T(8,128)(2,1)} %bitcast.8, bf16[2,32,512]{2,1,0:T(8,128)(2,1)} %bitcast.10), custom_call_target="tpu_custom_call" | custom-call | flops 99999997952 | bytes 1 | tf_op jit(solution)/shard_map/pallas_call | solution.py:435
  9.8 0.7 %collective-permute-done.2.got = bf16[3968,128]{1,0:T(8,128)(2,1)} collective-permute-done((bf16[3968,128]{1,0:T(8,128)(2,1)S(1)}, bf16[3968,128]{1,0:T(8,128)(2,1)}, u32[]{:S(2)}, u32[]{:S(2)}) %collective-permute-start.2) | collective-permute-done | bytes 1015840 | tf_op jit(solution)/shard_map/ppermute | solution.py:433
  10.5 3.5 %shard_map.97 = (f32[2,1024,256]{2,1,0:T(8,128)S(1)}, bf16[2,256,1024]{2,1,0:T(8,128)(2,1)S(1)}, bf16[4,256,512]{2,1,0:T(8,128)(2,1)S(1)}, bf16[4,512,256]{2,1,0:T(8,128)(2,1)S(1)}, bf16[384,256]{1,0:T(8,128)(2,1)S(1)}) custom-call(s32[1]{0:T(128)} %bitcast.core, bf16[2,512,128]{2,1,0:T(8,128)(2,1)} %left.5, bf16[2,512,128]{2,1,0:T(8,128)(2,1)} %right.5, ...), custom_call_target="tpu_custom_call" | custom-call | flops 1 | bytes 1 | tf_op jit(solution)/shard_map/pallas_call | solution.py:454
  14.0 2.7 %collective-permute-done.1.halo_same = bf16[2,512,128]{2,1,0:T(8,128)(2,1)S(1)} collective-permute-done((bf16[2,512,128]{2,1,0:T(8,128)(2,1)S(1)}, bf16[2,512,128]{2,1,0:T(8,128)(2,1)S(1)}, u32[]{:S(2)}, u32[]{:S(2)}) %collective-permute-start.1) | collective-permute-done | bytes 262176 | tf_op jit(solution)/shard_map/ppermute | solution.py:432
  16.8 0.0 collective-permute-done.halo_other
  16.8 4.2 %shard_map.98 = (bf16[2,1024,256]{2,1,0:T(8,128)(2,1)S(1)}, bf16[2,512,128]{2,1,0:T(8,128)(2,1)}, bf16[2,512,128]{2,1,0:T(8,128)(2,1)}, f32[8,48,384]{2,1,0:T(8,128)S(1)}, bf16[7,512,128]{2,1,0:T(8,128)(2,1)S(1)}) custom-call(s32[1]{0:T(128)} %bitcast.core, s32[1]{0:T(128)} %bitcast.1.chip, bf16[2,512,128]{2,1,0:T(8,128)(2,1)S(1)} %collective-permute-done.halo_other, ...), custom_call_target="tpu_custom_call" | custom-call | flops 1 | bytes 1 | tf_op jit(solution)/shard_map/pallas_call | solution.py:485
  20.9 0.4 collective-permute-start.3
  21.3 1.5 %collective-permute-start.4 = (bf16[2,512,128]{2,1,0:T(8,128)(2,1)}, bf16[2,512,128]{2,1,0:T(8,128)(2,1)S(1)}, u32[]{:S(2)}, u32[]{:S(2)}) collective-permute-start(bf16[2,512,128]{2,1,0:T(8,128)(2,1)} %get-tuple-element.31), channel_id=1, source_target_pairs={{1,2},{2,1},{3,4},{4,3},{5,6},{6,5},{7,8},{8,7},{9,10},{10,9},{11,... | collective-permute-start | bytes 786440 | tf_op jit(solution)/shard_map/ppermute | solution.py:509
  22.8 0.9 %collective-permute-start.5 = (bf16[2,512,128]{2,1,0:T(8,128)(2,1)}, bf16[2,512,128]{2,1,0:T(8,128)(2,1)S(1)}, u32[]{:S(2)}, u32[]{:S(2)}) collective-permute-start(bf16[2,512,128]{2,1,0:T(8,128)(2,1)} %get-tuple-element.32), channel_id=1, source_target_pairs={{2,0},{1,3},{4,2},{3,5},{6,4},{5,7},{8,6},{7,9},{10,8},{9,11},{12,... | collective-permute-start | bytes 786440 | tf_op jit(solution)/shard_map/ppermute | solution.py:510
  23.8 0.0 collective-permute-done.3._.across
  23.8 0.8 %shard_map.101 = bf16[8,48,384]{2,1,0:T(8,128)(2,1)} custom-call(f32[8,48,384]{2,1,0:T(8,128)S(1)} %get-tuple-element.35.keep, bf16[7,512,128]{2,1,0:T(8,128)(2,1)S(1)} %collective-permute-done.3._.across), custom_call_target="tpu_custom_call" | custom-call | flops 1 | bytes 1 | tf_op jit(solution)/shard_map/pallas_call | solution.py:513
  24.6 6.2 %all-to-all-start = ((bf16[8,48,384]{2,1,0:T(8,128)(2,1)}), bf16[8,48,384]{2,1,0:T(8,128)(2,1)S(1)}, u32[]{:S(2)}, u32[]{:S(2)}) async-start(bf16[8,48,384]{2,1,0:T(8,128)(2,1)} %shard_map.101), calls=%async_computation | async-start | bytes 589824 | tf_op jit(solution)/shard_map/all_to_all | solution.py:528
  30.7 0.8 %shard_map.99.keep = f32[4,512,128]{2,1,0:T(8,128)S(1)} custom-call(s32[1]{0:T(128)} %bitcast.core, bf16[2,1024,256]{2,1,0:T(8,128)(2,1)S(1)} %get-tuple-element.29.whole_grad, bf16[768,384]{1,0:T(8,128)(2,1)S(1)} %get-tuple-element.28.taps, bf16[7,512,128]{2,1,0:T(8,128)(2,1)S(1)} %collective-permute-done.3._.across), custom_call_target="tpu_custom_call" | custom-call | flops 1 | bytes 1 | tf_op jit(solution)/shard_map/pallas_call | solution.py:529
  31.6 0.0 collective-permute-done.4.edge_other
  31.6 0.0 collective-permute-done.5.edge_same
  31.6 0.9 %shard_map.100 = (bf16[2,512,128]{2,1,0:T(8,128)(2,1)}, bf16[2,512,128]{2,1,0:T(8,128)(2,1)}, f32[8,128]{1,0:T(8,128)S(1)}) custom-call(s32[1]{0:T(128)} %bitcast.core, s32[1]{0:T(128)} %bitcast.1.chip, f32[4,512,128]{2,1,0:T(8,128)S(1)} %shard_map.99.keep, bf16[7,512,128]{2,1,0:T(8,128)(2,1)S(1)} %collective-permute-done.3._.across, ...), custom_call_target="tpu_custom_call" | custom-call | flops 99999997952 | bytes 1 | tf_op jit(solution)/shard_map/pallas_call | solution.py:541
  32.5 7.6 %all-to-all-done.parts = bf16[8,48,384]{2,1,0:T(8,128)(2,1)S(1)} async-done(((bf16[8,48,384]{2,1,0:T(8,128)(2,1)}), bf16[8,48,384]{2,1,0:T(8,128)(2,1)S(1)}, u32[]{:S(2)}, u32[]{:S(2)}) %all-to-all-start) | async-done | bytes 294944 | tf_op jit(solution)/shard_map/all_to_all | solution.py:528
  40.1 0.1 collective-permute-start.6
  40.2 1.3 %collective-permute-done.6.got = f32[48,384]{1,0:T(8,128)S(1)} collective-permute-done((f32[48,384]{1,0:T(8,128)S(1)}, f32[48,384]{1,0:T(8,128)S(1)}, u32[]{:S(2)}, u32[]{:S(2)}) %collective-permute-start.6) | collective-permute-done | bytes 73760 | tf_op jit(solution)/shard_map/ppermute | solution.py:562
  41.5 0.7 %shard_map.103 = f32[32,1152]{1,0:T(8,128)} custom-call(s32[1]{0:T(128)} %bitcast.core, f32[48,384]{1,0:T(8,128)S(1)} %shard_map.102.mine, f32[48,384]{1,0:T(8,128)S(1)} %collective-permute-done.6.got), custom_call_target="tpu_custom_call" | custom-call | flops 1 | bytes 1 | tf_op jit(solution)/shard_map/pallas_call | solution.py:564
  (1 shorter events, 0.0 us)
Async XLA Ops:
  1.8 15.0 %collective-permute-start.1 = (bf16[2,512,128]{2,1,0:T(8,128)(2,1)S(1)}, bf16[2,512,128]{2,1,0:T(8,128)(2,1)S(1)}, u32[]{:S(2)}, u32[]{:S(2)}) collective-permute-start(bf16[2,512,128]{2,1,0:T(8,128)(2,1)S(1)} %get-tuple-element.21), channel_id=1, source_target_pairs={{0,2},{3,1},{2,4},{5,3},{4,6},{7,5},{6,8},{9,7},{8,10},{11,9},{10,... | collective-permute-start | bytes 786440 | tf_op jit(solution)/shard_map/ppermute | solution.py:432
  4.8 12.0 %collective-permute-start = (bf16[2,512,128]{2,1,0:T(8,128)(2,1)S(1)}, bf16[2,512,128]{2,1,0:T(8,128)(2,1)S(1)}, u32[]{:S(2)}, u32[]{:S(2)}) collective-permute-start(bf16[2,512,128]{2,1,0:T(8,128)(2,1)S(1)} %get-tuple-element.20._), channel_id=1, source_target_pairs={{1,2},{2,1},{3,4},{4,3},{5,6},{6,5},{7,8},{8,7},{9,10},{10,9},{11,... | collective-permute-start | bytes 786440 | tf_op jit(solution)/shard_map/ppermute | solution.py:431
  7.7 2.8 %collective-permute-start.2 = (bf16[3968,128]{1,0:T(8,128)(2,1)S(1)}, bf16[3968,128]{1,0:T(8,128)(2,1)}, u32[]{:S(2)}, u32[]{:S(2)}) collective-permute-start(bf16[3968,128]{1,0:T(8,128)(2,1)S(1)} %shard_map.95), channel_id=1, source_target_pairs={{0,1},{1,0},{2,3},{3,2},{4,5},{5,4},{6,7},{7,6},{8,9},{9,8},{10,11... | collective-permute-start | bytes 3047432 | tf_op jit(solution)/shard_map/ppermute | solution.py:433
  20.9 2.8 %collective-permute-start.3 = (bf16[7,512,128]{2,1,0:T(8,128)(2,1)S(1)}, bf16[7,512,128]{2,1,0:T(8,128)(2,1)S(1)}, u32[]{:S(2)}, u32[]{:S(2)}) collective-permute-start(bf16[7,512,128]{2,1,0:T(8,128)(2,1)S(1)} %get-tuple-element.30), channel_id=1, source_target_pairs={{0,1},{1,0},{2,3},{3,2},{4,5},{5,4},{6,7},{7,6},{8,9},{9,8},{10,11... | collective-permute-start | bytes 2752520 | tf_op jit(solution)/shard_map/ppermute | solution.py:511
  21.3 10.3 %collective-permute-start.4 = (bf16[2,512,128]{2,1,0:T(8,128)(2,1)}, bf16[2,512,128]{2,1,0:T(8,128)(2,1)S(1)}, u32[]{:S(2)}, u32[]{:S(2)}) collective-permute-start(bf16[2,512,128]{2,1,0:T(8,128)(2,1)} %get-tuple-element.31), channel_id=1, source_target_pairs={{1,2},{2,1},{3,4},{4,3},{5,6},{6,5},{7,8},{8,7},{9,10},{10,9},{11,... | collective-permute-start | bytes 786440 | tf_op jit(solution)/shard_map/ppermute | solution.py:509
  22.8 8.7 %collective-permute-start.5 = (bf16[2,512,128]{2,1,0:T(8,128)(2,1)}, bf16[2,512,128]{2,1,0:T(8,128)(2,1)S(1)}, u32[]{:S(2)}, u32[]{:S(2)}) collective-permute-start(bf16[2,512,128]{2,1,0:T(8,128)(2,1)} %get-tuple-element.32), channel_id=1, source_target_pairs={{2,0},{1,3},{4,2},{3,5},{6,4},{5,7},{8,6},{7,9},{10,8},{9,11},{12,... | collective-permute-start | bytes 786440 | tf_op jit(solution)/shard_map/ppermute | solution.py:510
  24.6 15.5 %all-to-all-start = ((bf16[8,48,384]{2,1,0:T(8,128)(2,1)}), bf16[8,48,384]{2,1,0:T(8,128)(2,1)S(1)}, u32[]{:S(2)}, u32[]{:S(2)}) async-start(bf16[8,48,384]{2,1,0:T(8,128)(2,1)} %shard_map.101), calls=%async_computation | async-start | bytes 589824 | tf_op jit(solution)/shard_map/all_to_all | solution.py:528
  40.1 1.3 %collective-permute-start.6 = (f32[48,384]{1,0:T(8,128)S(1)}, f32[48,384]{1,0:T(8,128)S(1)}, u32[]{:S(2)}, u32[]{:S(2)}) collective-permute-start(f32[48,384]{1,0:T(8,128)S(1)} %shard_map.102.mine), channel_id=1, source_target_pairs={{0,1},{1,0},{2,3},{3,2},{4,5},{5,4},{6,7},{7,6},{8,9},{9,8},{10,11... | collective-permute-start | bytes 221192 | tf_op jit(solution)/shard_map/ppermute | solution.py:562
